TPU v7x, 32 devices: a whole 2x2x4 slice. The times are simulated.
32 devices in a mesh: tile: 8 (over y, x, core), head: 4 (over z).
Axes of the slice: x: 2, y: 2, z: 4, core: 2. Of those that a mesh axis runs over, the one named last changes fastest.
Arguments:
- tokens: bfloat16 [2048, 384], P('tile'), may hold values from -6 to 6
- ln_gain: float32 [384], replicated, may hold values from 0.1 to 1.9
- qkv_weight: bfloat16 [3, 768, 384], P(None, 'head'), may hold values from -0.3125 to 0.3125
- query_pool: bfloat16 [4, 768], P(None, 'head'), may hold values from -3 to 3
- key_pool: bfloat16 [16, 768], P(None, 'head'), may hold values from -1.5 to 1.5
- value_pool: bfloat16 [16, 768], P(None, 'head'), may hold values from -1.5 to 1.5
- proj_weight: bfloat16 [768, 768], P('head'), may hold values from -0.21875 to 0.21875
- skip_weight: bfloat16 [768, 384], P('head'), may hold values from -0.3125 to 0.3125
- cotangent: bfloat16 [512, 768], P('tile', 'head'), may hold values from -6 to 6
Outputs:
- block_out: bfloat16 [512, 768], P('tile', 'head')
- input_grad: bfloat16 [2048, 384], P('tile')
- qkv_grad: float32 [3, 768, 384], P(None, 'head')
- proj_grad: float32 [768, 768], P('head')
All inputs are finite; a program needn't handle non-finite values.
Results may differ from a plain program's by a relative error of at most 0.02.
Values may be sent and summed in bfloat16 or wider, within the bound.
A program may use at most 64 MiB of HBM per device.

v0:
```python
import jax
import jax.numpy as jnp
from jax import lax
from jax.sharding import PartitionSpec as P

HEAD_DIM = 96
TILE_H = 8
TILE_W = 32


EPSILON = 1e-06


def normalize(tokens):
    values_in = tokens.astype(jnp.float32)
    center = values_in - jnp.mean(values_in, axis=-1, keepdims=True)
    inv_std = lax.rsqrt(jnp.mean(center * center, axis=-1, keepdims=True) + EPSILON)
    return (center * inv_std, inv_std)


def pool_field(feature, weight, stride):
    channels = feature.shape[-1]
    cells_grid = feature.reshape(-1, TILE_H // stride, stride, TILE_W // stride, stride, channels)
    kernel = weight.astype(jnp.float32).reshape(stride, stride, channels)
    return jnp.einsum("fiajbc,abc->fijc", cells_grid, kernel).reshape(-1, channels)


def spread_field(upstream, weight, stride):
    channels = upstream.shape[-1]
    cells_grid = upstream.reshape(-1, TILE_H // stride, TILE_W // stride, channels)
    kernel = weight.astype(jnp.float32).reshape(stride, stride, channels)
    return jnp.einsum("fijc,abc->fiajbc", cells_grid, kernel).reshape(-1, channels)


def mean_pool(tokens):
    channels = tokens.shape[-1]
    cells_grid = tokens.astype(jnp.float32).reshape(-1, TILE_H // 2, 2, TILE_W // 2, 2, channels)
    return jnp.sum(cells_grid, axis=(2, 4)).reshape(-1, channels) * 0.25


def expand_rows(upstream):
    channels = upstream.shape[-1]
    cells_grid = upstream.reshape(-1, TILE_H // 2, 1, TILE_W // 2, 1, channels)
    cells_grid = jnp.broadcast_to(
        cells_grid, (cells_grid.shape[0], TILE_H // 2, 2, TILE_W // 2, 2, channels)
    )
    return cells_grid.reshape(-1, channels)


def norm_back(upstream, unit_rows, inv_std, ln_gain):
    scaled = upstream * ln_gain
    return inv_std * (
        scaled
        - jnp.mean(scaled, axis=-1, keepdims=True)
        - unit_rows * jnp.mean(scaled * unit_rows, axis=-1, keepdims=True)
    )


def attend(operands):
    queries, grad_rows, key_rows, value_rows = operands
    scale = HEAD_DIM ** (-0.5)
    scores = jnp.dot(queries, key_rows.T, preferred_element_type=jnp.float32) * scale
    exp_scores = jnp.exp(scores)
    row_total = jnp.sum(exp_scores, axis=-1, keepdims=True)
    attn_probs = (exp_scores / row_total).astype(jnp.bfloat16)
    out_rows = (
        jnp.dot(attn_probs, value_rows, preferred_element_type=jnp.float32)
        + queries.astype(jnp.float32)
    ).astype(jnp.bfloat16)
    dprobs = jnp.dot(grad_rows, value_rows.T, preferred_element_type=jnp.float32)
    probs_wide = attn_probs.astype(jnp.float32)
    row_delta = jnp.sum(probs_wide * dprobs, axis=-1, keepdims=True)
    d_scores = (scale * probs_wide * (dprobs - row_delta)).astype(jnp.bfloat16)
    dquery = jnp.dot(d_scores, key_rows, preferred_element_type=jnp.float32) + grad_rows.astype(
        jnp.float32
    )
    key_grad = jnp.dot(d_scores.T, queries, preferred_element_type=jnp.float32)
    value_grad = jnp.dot(attn_probs.T, grad_rows, preferred_element_type=jnp.float32)
    return (out_rows, dquery, key_grad, value_grad, row_total[:, 0], row_delta[:, 0])


def split_heads(rows_in):
    return rows_in.reshape(rows_in.shape[0], -1, HEAD_DIM).transpose(1, 0, 2)


def join_heads(stacked):
    return stacked.transpose(1, 0, 2).reshape(stacked.shape[1], -1)


def local(
    tokens,
    ln_gain,
    qkv_weight,
    query_pool,
    key_pool,
    value_pool,
    proj_weight,
    skip_weight,
    cotangent,
):
    unit_rows, inv_std = normalize(tokens)
    normed = (unit_rows * ln_gain).astype(jnp.bfloat16)
    projected = [
        jnp.dot(normed, qkv_weight[which].T, preferred_element_type=jnp.float32)
        for which in range(3)
    ]
    query_pooled = pool_field(projected[0], query_pool, 2).astype(jnp.bfloat16)
    key_pooled = pool_field(projected[1], key_pool, 4).astype(jnp.bfloat16)
    value_pooled = pool_field(projected[2], value_pool, 4).astype(jnp.bfloat16)
    all_keys, all_values = (
        lax.all_gather(key_pooled, "tile", axis=0, tiled=True),
        lax.all_gather(value_pooled, "tile", axis=0, tiled=True),
    )
    full_cotangent = lax.all_gather(cotangent, "head", axis=1, tiled=True)
    d_attended = jnp.dot(full_cotangent, proj_weight.T, preferred_element_type=jnp.float32).astype(
        jnp.bfloat16
    )
    head_outs, query_grads, key_grads, value_grads, row_totals, row_deltas = lax.map(
        attend,
        (
            split_heads(query_pooled),
            split_heads(d_attended),
            split_heads(all_keys),
            split_heads(all_values),
        ),
    )
    attended = join_heads(head_outs)
    head_part = jnp.dot(attended, proj_weight, preferred_element_type=jnp.float32)
    summed = lax.psum_scatter(
        head_part.astype(jnp.bfloat16), "head", scatter_dimension=1, tiled=True
    ).astype(jnp.float32)
    pooled_input = mean_pool(tokens).astype(jnp.bfloat16)
    block_out = (
        summed + jnp.dot(pooled_input, skip_weight.T, preferred_element_type=jnp.float32)
    ).astype(jnp.bfloat16)
    proj_part = jnp.dot(attended.T, full_cotangent, preferred_element_type=jnp.float32)
    d_pooled_part = jnp.dot(cotangent, skip_weight, preferred_element_type=jnp.float32)
    own_keys, own_values = (
        lax.psum_scatter(key_grads, "tile", scatter_dimension=1, tiled=True),
        lax.psum_scatter(value_grads, "tile", scatter_dimension=1, tiled=True),
    )
    d_projected = jnp.stack(
        [
            spread_field(join_heads(query_grads), query_pool, 2),
            spread_field(join_heads(own_keys), key_pool, 4),
            spread_field(join_heads(own_values), value_pool, 4),
        ]
    ).astype(jnp.bfloat16)
    qkv_part = jnp.stack(
        [
            jnp.dot(d_projected[which].T, normed, preferred_element_type=jnp.float32)
            for which in range(3)
        ]
    )
    qkv_grad, proj_grad = lax.psum((qkv_part, proj_part), "tile")
    d_normed_part = jnp.dot(d_projected[0], qkv_weight[0], preferred_element_type=jnp.float32)
    d_normed_part = d_normed_part + jnp.dot(
        d_projected[1], qkv_weight[1], preferred_element_type=jnp.float32
    )
    d_normed_part = d_normed_part + jnp.dot(
        d_projected[2], qkv_weight[2], preferred_element_type=jnp.float32
    )
    d_normed, d_pooled = (
        lax.psum(d_normed_part.astype(jnp.bfloat16), "head").astype(jnp.float32),
        lax.psum(d_pooled_part.astype(jnp.bfloat16), "head").astype(jnp.float32),
    )
    input_grad = (
        norm_back(d_normed, unit_rows, inv_std, ln_gain) + expand_rows(d_pooled) * 0.25
    ).astype(jnp.bfloat16)
    return (block_out, input_grad, qkv_grad, proj_grad)


def solution(mesh):
    placed = (
        P("tile", None),
        P(),
        P(None, "head", None),
        P(None, "head"),
        P(None, "head"),
        P(None, "head"),
        P("head", None),
        P("head", None),
        P("tile", "head"),
    )
    return jax.shard_map(
        local,
        mesh=mesh,
        in_specs=placed,
        out_specs=(P("tile", "head"), P("tile", None), P(None, "head", None), P("head", None)),
        check_vma=False,
    )
```

profile of v0, /device:TPU:0, one launch (start us, length us, event | category | flops | bytes accessed | tf_op | source)
XLA Modules:
  0.0 216.3 jit_solution(16118410419892626590)
XLA Ops:
  8.1 1.1 convert_reduce_fusion
  9.4 0.7 copy-done.7
  10.4 0.6 copy-done.10
  11.1 0.7 copy-done.9
  11.8 0.7 copy-done.6
  12.6 15.0 %all-gather = bf16[4,192,64]{1,2,0:T(8,128)(2,1)S(1)} all-gather(bf16[1,192,64]{1,2,0:T(8,128)(2,1)S(1)} %bitcast.249), channel_id=1, replica_groups=mesh['tile'=8,'head'=4] {'head'}, dimensions={0}, use_global_device_ids=true | all-gather | bytes 122880 | tf_op jit(solution)/shard_map/all_gather | solution.py:114
  28.2 0.5 copy-done.5
  28.7 0.3 fusion.40
  29.1 0.3 fusion.39
  29.4 9.2 %all_gather.10 = bf16[128,192]{1,0:T(8,128)(2,1)S(1)} all-gather(bf16[16,192]{1,0:T(8,128)(2,1)S(1)} %bitcast.258), channel_id=1, replica_groups=mesh['tile'=8,'head'=4] {'tile'}, dimensions={0}, use_global_device_ids=true | all-gather | bytes 55296 | tf_op jit(solution)/shard_map/all_gather | solution.py:112
  38.7 9.2 %all_gather.9 = bf16[128,192]{1,0:T(8,128)(2,1)S(1)} all-gather(bf16[16,192]{1,0:T(8,128)(2,1)S(1)} %bitcast.257), channel_id=1, replica_groups=mesh['tile'=8,'head'=4] {'tile'}, dimensions={0}, use_global_device_ids=true | all-gather | bytes 55296 | tf_op jit(solution)/shard_map/all_gather | solution.py:111
  48.4 2.6 %while.16 = (s32[]{:T(128)}, bf16[2,64,96]{2,1,0:T(8,128)(2,1)S(1)}, f32[2,64,96]{2,1,0:T(8,128)S(1)}, f32[2,128,96]{1,2,0:T(8,128)S(1)}, f32[2,128,96]{1,2,0:T(...) while((s32[]{:T(128)}, ...), condition=%wide.region_5.6_spmd, body=%wide.region_2.5_spmd.sunk | while | flops 9566082 | bytes 597357 | solution.py:118
  51.0 0.8 copy.40
  51.8 0.8 copy.39
  52.9 0.8 copy.65
  54.9 1.1 fusion.61
  56.1 20.6 %psum.29 = bf16[64,384]{1,0:T(8,128)(2,1)S(1)} all-reduce(bf16[64,384]{1,0:T(8,128)(2,1)S(1)} %convolution_convert_fusion.1), channel_id=1, replica_groups=mesh['tile'=8,'head'=4] {'head'}, use_global_device_ids=true, to_apply=%region_13.14 | all-reduce | flops 24576 | bytes 98304 | tf_op jit(solution)/shard_map/psum | solution.py:165
  77.1 0.3 reduce_sum.65
  77.5 0.6 copy-done.11
  78.1 0.6 dynamic-slice
  79.3 27.5 %all-reduce.12.cloned.1.call-done = (f32[2,128,96]{2,0,1:T(2,128)}, f32[2,128,96]{2,0,1:T(2,128)}) async-done(((f32[2,128,96]{2,0,1:T(2,128)}, f32[2,128,96]{2,0,1:T(2,128)}), (f32[2,128,96]{2,0,1:T(2,128)}, f32[2,128,96]{2,0,1:T(2,128)})) %all-reduce.12.cloned.1.call-update) | async-done | bytes 196624
  106.8 0.7 dynamic-slice_bitcast_fusion
  108.5 0.9 fusion.34
  109.7 1.0 pad_maximum_fusion
  110.7 0.9 copy.66
  111.6 0.8 fusion.41
  112.4 31.2 %all-reduce.8.cloned.1.call-done = bf16[256,384]{1,0:T(8,128)(2,1)} async-done(((bf16[256,384]{1,0:T(8,128)(2,1)}), bf16[256,384]{1,0:T(8,128)(2,1)}) %all-reduce.8.cloned.1.call-update) | async-done | bytes 196624 | tf_op jit(solution)/shard_map/psum | solution.py:164
  143.6 1.2 fusion.42
  144.9 0.9 add_convert_fusion
  145.8 59.9 %all-reduce.10.cloned.1.call-done = (f32[3,192,384]{2,1,0:T(8,128)}, f32[192,768]{1,0:T(8,128)}) async-done(((f32[3,192,384]{2,1,0:T(8,128)}, f32[192,768]{1,0:T(8,128)}), (f32[3,192,384]{2,1,0:T(8,128)}, f32[192,768]{1,0:T(8,128)})) %all-reduce.10.cloned.1.call-update) | async-done | bytes 1474576 | tf_op jit(solution)/shard_map/psum | solution.py:155
  205.7 2.2 %copy.102 = f32[3,192,384]{2,1,0:T(8,128)} copy(f32[3,192,384]{2,1,0:T(8,128)} %get-tuple-element.210) | data formatting | bytes 1769472
  207.9 0.8 copy.103
  (93 shorter events, 7.6 us)
Async XLA Ops:
  8.0 19.9 %copy-start = (bf16[192,768]{1,0:T(8,128)(2,1)S(1)}, bf16[192,768]{1,0:T(8,128)(2,1)}, u32[]{:S(2)}) copy-start(bf16[192,768]{1,0:T(8,128)(2,1)} %param.17) | copy-start | bytes 884740
  8.0 1.2 copy-start.1
  8.0 98.8 %all-reduce.12.cloned.1.call-start = ((), (), s32[]{:S(2)}) async-start(), calls=%async_computation.4 | async-start | bytes 524288
  9.4 0.7 copy-start.7
  10.3 0.7 copy-start.10
  10.4 0.7 copy-start.8
  11.1 0.7 copy-start.9
  11.8 0.8 copy-start.6
  27.7 1.0 copy-start.5
  52.6 58.2 %reduce-scatter.4.cloned.1.call-start = ((), (), s32[]{:S(2)}) async-start(), calls=%async_computation.2 | async-start | bytes 245760
  53.8 89.8 %all-reduce.8.cloned.1.call-start = ((), (), s32[]{:S(2)}) async-start(), calls=%async_computation.1 | async-start | bytes 393216 | tf_op jit(solution)/shard_map/psum | solution.py:164
  54.9 1.1 copy-start.4
  77.4 0.7 copy-start.11
  109.4 96.3 %all-reduce.10.cloned.1.call-start = ((), (), s32[]{:S(2)}) async-start(), calls=%async_computation.3 | async-start | bytes 2949120 | tf_op jit(solution)/shard_map/psum | solution.py:155
  143.6 1.3 copy-start.2
  205.7 2.2 %copy-start.3 = (f32[192,768]{1,0:T(8,128)S(1)}, f32[192,768]{1,0:T(8,128)}, u32[]{:S(2)}) copy-start(f32[192,768]{1,0:T(8,128)} %get-tuple-element.211) | copy-start | bytes 1769476
Sparse Core Ops, SparseCore 0:
  52.7 54.0 all-reduce.11
Sparse Core Ops, SparseCore 1:
  55.9 19.9 reduce-scatter.3
  109.5 34.0 all-reduce.7
  147.8 57.9 all-reduce.9
where the time goes:
time: 217 us; the launch traced here: 216 us
  waiting for transfers between devices  119 us (55%)
  blocking collectives  54.1 us (25%)
  between operations  16.7 us (8%)
  local copies, waits for them, and re-layouts  13.6 us (6%)
  matrix products  7.79 us (4%)
  other arithmetic  5.19 us (2%)
    psum x1, waiting for transfers between devices, local(): qkv_grad, proj_grad = lax.psum((qkv_part, proj_part), 'tile')  59.9 us
    psum x1, waiting for transfers between devices, local(): lax.psum(d_normed_part.astype(jnp.bfloat16), 'head').astype(jnp.float32)  31.2 us
    unnamed x6, waiting for transfers between devices  27.6 us
    psum x1, blocking collectives, local(): lax.psum(d_pooled_part.astype(jnp.bfloat16), 'head').astype(jnp.float32)  20.6 us
    all_gather x1, blocking collectives, local(): full_cotangent = lax.all_gather(cotangent, 'head', axis=1, tiled=True)  15 us
    unnamed x30, local copies, waits for them, and re-layouts  9.38 us
    all_gather x1, blocking collectives, local(): lax.all_gather(value_pooled, 'tile', axis=0, tiled=True)  9.24 us
    all_gather x1, blocking collectives, local(): lax.all_gather(key_pooled, 'tile', axis=0, tiled=True)  9.2 us
  transfers between devices with their start and end apart: 4, of which 3 were waited for; matrix products, arithmetic and copies ran while one was open for 6% of the time, Pallas kernels for 0%

commit v1 on v0

v1 whole, which is shorter than its diff:
```python
import functools

import jax
import jax.numpy as jnp
from jax import lax
from jax.experimental import pallas as pl
from jax.experimental.pallas import tpu as pltpu
from jax.sharding import PartitionSpec as P

HEAD_DIM = 96
TILE_H = 8
TILE_W = 32
EPSILON = 1e-06
SLAB = TILE_H * TILE_W // 16
CELLS = SLAB * 4
MESH = pl.DeviceIdType.MESH
F32 = jnp.float32
BF16 = jnp.bfloat16


def mm(a, b, contract=(1, 0)):
    return lax.dot_general(
        a, b, (((contract[0],), (contract[1],)), ((), ())), preferred_element_type=F32
    )


def token_order(shape, dim):
    p = lax.broadcasted_iota(jnp.int32, shape, dim)
    slab, block = p >> 4, p & 15
    a, b = slab >> 2, slab & 3
    return ((block >> 3) * 4 + a) * TILE_W + (block & 7) * 4 + b


def cell_order(shape, dim):
    p = lax.broadcasted_iota(jnp.int32, shape, dim)
    slab, block = p >> 4, p & 15
    a, b = slab >> 1, slab & 1
    return ((block >> 3) * 2 + a) * (TILE_W // 2) + (block & 7) * 2 + b


def one_hot(order, size, transposed=False):
    shape = (size, size)
    dim = 1 if transposed else 0
    other = lax.broadcasted_iota(jnp.int32, shape, 1 - dim)
    return jnp.where(order(shape, dim) == other, 1.0, 0.0).astype(BF16)


def rows(start, size):
    return pl.ds(pl.multiple_of(start, 16), size)


def kernel(
    n,
    nh,
    share_a,
    share_b,
    tokens_ref,
    gain_ref,
    qkv_ref,
    qpool_ref,
    kpool_ref,
    vpool_ref,
    proj_ref,
    skip_ref,
    cot_ref,
    block_out_ref,
    input_grad_ref,
    qkv_grad_ref,
    proj_grad_ref,
    cot_all,
    kv_all,
    kvg_send,
    kvg_recv,
    dp_send,
    dp_recv,
    hp_send,
    hp_recv,
    ga_send,
    ga_recv,
    ga_out,
    gb_send,
    gb_recv,
    gb_out,
    dn_send,
    dn_recv,
    ig_all,
    unit_ref,
    inv_ref,
    tile_send,
    tile_recv,
    head_send,
    head_recv,
):
    me = lax.axis_index("tile")
    my_head = lax.axis_index("head")
    chans = qkv_ref.shape[1]
    wide = qkv_ref.shape[2]
    share_h = unit_ref.shape[0] // nh

    def at_tile(k):
        return (lax.rem(me + k, n), my_head)

    def at_head(k):
        return (me, lax.rem(my_head + k, nh))

    def send_tile(stage, k, src, dst, device):
        copy = pltpu.make_async_remote_copy(
            src_ref=src,
            dst_ref=dst,
            send_sem=tile_send.at[stage, k],
            recv_sem=tile_recv.at[stage, k],
            device_id=device,
            device_id_type=MESH,
        )
        copy.start()
        return copy

    def send_head(stage, k, src, dst, device):
        copy = pltpu.make_async_remote_copy(
            src_ref=src,
            dst_ref=dst,
            send_sem=head_send.at[stage, k],
            recv_sem=head_recv.at[stage, k],
            device_id=device,
            device_id_type=MESH,
        )
        copy.start()
        return copy

    started = []

    def arrived(copies):
        for copy in copies:
            copy.wait_recv()
        started.extend(copies)

    barrier = pltpu.get_barrier_semaphore()
    for k in range(1, n):
        pl.semaphore_signal(barrier, inc=1, device_id=at_tile(k), device_id_type=MESH)
    for k in range(1, nh):
        pl.semaphore_signal(barrier, inc=1, device_id=at_head(k), device_id_type=MESH)

    order = one_hot(token_order, TILE_H * TILE_W)
    tokens = mm(order, tokens_ref[...])
    center = tokens - jnp.mean(tokens, axis=-1, keepdims=True)
    inv_std = lax.rsqrt(jnp.mean(center * center, axis=-1, keepdims=True) + EPSILON)
    unit = center * inv_std
    unit_ref[...] = unit
    inv_ref[...] = jnp.broadcast_to(inv_std, inv_ref.shape)
    gain = gain_ref[...]
    normed = (unit * gain).astype(BF16)

    kpool = kpool_ref[...].astype(F32)
    vpool = vpool_ref[...].astype(F32)
    qpool = qpool_ref[...].astype(F32)

    def pool_block(field, pool):
        total = pool[0:1] * field[0:SLAB]
        for s in range(1, 16):
            total = total + pool[s : s + 1] * field[s * SLAB : (s + 1) * SLAB]
        return total

    kv_all[0, 0:SLAB, :] = pool_block(mm(normed, qkv_ref[1], (1, 1)), kpool).astype(BF16)
    kv_all[1, 0:SLAB, :] = pool_block(mm(normed, qkv_ref[2], (1, 1)), vpool).astype(BF16)

    pl.semaphore_wait(barrier, n + nh - 2)
    kv_copies = [
        send_tile(
            0,
            k,
            kv_all.at[:, 0:SLAB],
            kv_all.at[:, k * SLAB : (k + 1) * SLAB],
            at_tile(k),
        )
        for k in range(1, n)
    ]
    cot_copies = [
        send_head(0, k, cot_ref, cot_all.at[my_head], at_head(k)) for k in range(1, nh)
    ]
    cot_all[my_head] = cot_ref[...]

    def cell_slabs(a, b):
        return [
            (2 * a2 + b2, (2 * a + a2) * 4 + 2 * b + b2) for a2 in range(2) for b2 in range(2)
        ]

    field = mm(normed, qkv_ref[0], (1, 1))
    query_parts = []
    input_parts = []
    for a in range(2):
        for b in range(2):
            total = None
            whole = None
            for w, s in cell_slabs(a, b):
                term = qpool[w : w + 1] * field[s * SLAB : (s + 1) * SLAB]
                total = term if total is None else total + term
                piece = tokens[s * SLAB : (s + 1) * SLAB]
                whole = piece if whole is None else whole + piece
            query_parts.append(total)
            input_parts.append(whole)
    queries_wide = jnp.concatenate(query_parts, axis=0).astype(BF16).astype(F32)
    pooled_input = (jnp.concatenate(input_parts, axis=0) * 0.25).astype(BF16)

    cells = one_hot(cell_order, CELLS)
    cells_back = one_hot(cell_order, CELLS, transposed=True)
    pooled_input = mm(cells_back, pooled_input).astype(BF16)
    skipped = mm(pooled_input, skip_ref[...], (1, 1))

    own_cot = mm(cells, cot_ref[...]).astype(BF16)
    d_pooled = mm(own_cot, skip_ref[...]).astype(BF16)
    half = CELLS // 2
    dp_send[0] = d_pooled[:half]
    dp_send[1] = d_pooled[half:]
    dp_copies = [
        send_head(
            1,
            k,
            dp_send.at[lax.rem(my_head + k, nh) * 2 // nh],
            dp_recv.at[k],
            at_head(k),
        )
        for k in range(1, nh)
    ]

    arrived(cot_copies)
    full_cot = jnp.concatenate([cot_all[h] for h in range(nh)], axis=1)
    full_cot = mm(cells, full_cot).astype(BF16)
    d_attended = mm(full_cot, proj_ref[...], (1, 1)).astype(BF16).astype(F32)

    heads = chans // HEAD_DIM
    lane = lax.broadcasted_iota(jnp.int32, (CELLS, chans), 1)
    masks = [
        jnp.logical_and(lane >= h * HEAD_DIM, lane < (h + 1) * HEAD_DIM) for h in range(heads)
    ]

    def by_head(x):
        return jnp.concatenate([jnp.where(m, x, 0.0) for m in masks], axis=0).astype(BF16)

    def from_heads(x):
        total = jnp.where(masks[0], x[:CELLS], 0.0)
        for h in range(1, heads):
            total = jnp.where(masks[h], x[h * CELLS : (h + 1) * CELLS], total)
        return total

    q_rows = by_head(queries_wide)
    g_rows = by_head(d_attended)

    arrived(kv_copies)
    keys = kv_all[0]
    values = kv_all[1]
    scale = HEAD_DIM ** (-0.5)
    exp_scores = jnp.exp(mm(q_rows, keys, (1, 1)) * scale)
    row_total = jnp.sum(exp_scores, axis=-1, keepdims=True)
    probs = (exp_scores / row_total).astype(BF16)
    dprobs = mm(g_rows, values, (1, 1))
    probs_wide = probs.astype(F32)
    row_delta = jnp.sum(probs_wide * dprobs, axis=-1, keepdims=True)
    d_scores = (scale * probs_wide * (dprobs - row_delta)).astype(BF16)
    key_grad = mm(d_scores, q_rows, (0, 0))
    value_grad = mm(probs, g_rows, (0, 0))
    kvg_send[0] = key_grad.astype(BF16)
    kvg_send[1] = value_grad.astype(BF16)
    kvg_copies = [
        send_tile(
            1,
            k,
            kvg_send.at[:, k * SLAB : (k + 1) * SLAB],
            kvg_recv.at[:, k * SLAB : (k + 1) * SLAB],
            at_tile(n - k),
        )
        for k in range(1, n)
    ]

    attended = (from_heads(mm(probs, values)) + queries_wide).astype(BF16)
    head_part = mm(mm(cells_back, attended).astype(BF16), proj_ref[...])
    for h in range(nh):
        hp_send[h] = head_part[:, h * chans : (h + 1) * chans].astype(BF16)
    hp_copies = [
        send_head(2, k, hp_send.at[lax.rem(my_head + k, nh)], hp_recv.at[k], at_head(k))
        for k in range(1, nh)
    ]

    query_grad = from_heads(mm(d_scores, keys)) + d_attended
    spread = []
    for s in range(16):
        a, b = s // 4, s % 4
        cell = (a // 2) * 2 + b // 2
        w = (a % 2) * 2 + b % 2
        spread.append(qpool[w : w + 1] * query_grad[cell * SLAB : (cell + 1) * SLAB])
    d_projected = jnp.concatenate(spread, axis=0).astype(BF16)
    ga_send[0:chans, :] = mm(d_projected, normed, (0, 0)).astype(BF16)
    proj_part = mm(attended, full_cot, (0, 0)).astype(BF16)
    halves = proj_part.shape[1] // wide
    for i in range(halves):
        ga_send[(i + 1) * chans : (i + 2) * chans, :] = proj_part[:, i * wide : (i + 1) * wide]
    filled = (halves + 1) * chans
    if ga_send.shape[0] > filled:
        ga_send[filled:, :] = jnp.zeros((ga_send.shape[0] - filled, wide), BF16)
    ga_copies = [
        send_tile(
            2,
            k,
            ga_send.at[rows(lax.rem(me + k, n) * share_a, share_a)],
            ga_recv.at[k],
            at_tile(k),
        )
        for k in range(1, n)
    ]
    d_normed = mm(d_projected, qkv_ref[0])

    arrived(kvg_copies)
    for j, pool, own in ((0, kpool, key_grad), (1, vpool, value_grad)):
        total = own[0:SLAB]
        for k in range(1, n):
            total = total + kvg_recv[j, k * SLAB : (k + 1) * SLAB, :].astype(F32)
        d_projected = jnp.concatenate([pool[s : s + 1] * total for s in range(16)], axis=0)
        d_projected = d_projected.astype(BF16)
        gb_send[j * chans : (j + 1) * chans, :] = mm(d_projected, normed, (0, 0)).astype(BF16)
        d_normed = d_normed + mm(d_projected, qkv_ref[j + 1])
    filled = 2 * chans
    if gb_send.shape[0] > filled:
        gb_send[filled:, :] = jnp.zeros((gb_send.shape[0] - filled, wide), BF16)
    gb_copies = [
        send_tile(
            3,
            k,
            gb_send.at[rows(lax.rem(me + k, n) * share_b, share_b)],
            gb_recv.at[k],
            at_tile(k),
        )
        for k in range(1, n)
    ]
    dn_send[...] = d_normed.astype(BF16)
    dn_copies = [
        send_head(
            3,
            k,
            dn_send.at[rows(lax.rem(my_head + k, nh) * share_h, share_h)],
            dn_recv.at[k],
            at_head(k),
        )
        for k in range(1, nh)
    ]

    def reduce_and_share(stage, copies, sent, received, out, share):
        arrived(copies)
        mine = rows(me * share, share)
        total = sent[mine, :].astype(F32)
        for k in range(1, n):
            total = total + received[k].astype(F32)
        out[mine, :] = total.astype(BF16)
        return [
            send_tile(stage, k, out.at[mine], out.at[mine], at_tile(k)) for k in range(1, n)
        ]

    ga_copies = reduce_and_share(4, ga_copies, ga_send, ga_recv, ga_out, share_a)

    arrived(hp_copies)
    summed = hp_send[my_head].astype(F32)
    for k in range(1, nh):
        summed = summed + hp_recv[k].astype(F32)
    block_out_ref[...] = (summed + skipped).astype(BF16)

    arrived(dp_copies)
    d_pooled = dp_send[my_head * 2 // nh].astype(F32)
    for k in range(1, nh):
        d_pooled = d_pooled + dp_recv[k].astype(F32)
    arrived(dn_copies)
    mine = rows(my_head * share_h, share_h)
    d_normed = dn_send[mine, :].astype(F32)
    for k in range(1, nh):
        d_normed = d_normed + dn_recv[k].astype(F32)
    scaled = d_normed * gain
    own_unit = unit_ref[mine, :]
    back = inv_ref[mine, :][:, 0:1] * (
        scaled
        - jnp.mean(scaled, axis=-1, keepdims=True)
        - own_unit * jnp.mean(scaled * own_unit, axis=-1, keepdims=True)
    )
    left, right = d_pooled[:SLAB], d_pooled[SLAB:]
    back = back + jnp.concatenate([left, left, right, right], axis=0) * 0.25
    ig_all[mine, :] = back.astype(BF16)
    ig_copies = [
        send_head(4, k, ig_all.at[mine], ig_all.at[mine], at_head(k)) for k in range(1, nh)
    ]

    gb_copies = reduce_and_share(5, gb_copies, gb_send, gb_recv, gb_out, share_b)

    arrived(ga_copies)
    qkv_grad_ref[0] = ga_out[0:chans, :]
    for i in range(halves):
        proj_grad_ref[:, i * wide : (i + 1) * wide] = ga_out[(i + 1) * chans : (i + 2) * chans, :]
    arrived(ig_copies)
    input_grad_ref[...] = mm(
        one_hot(token_order, TILE_H * TILE_W, transposed=True), ig_all[...]
    ).astype(BF16)
    arrived(gb_copies)
    qkv_grad_ref[1] = gb_out[0:chans, :]
    qkv_grad_ref[2] = gb_out[chans : 2 * chans, :]
    for copy in started:
        copy.wait_send()


def share_of(total, n):
    return -(-total // (n * 16)) * 16


def local(n, nh, *operands):
    tokens, ln_gain, qkv, qpool, kpool, vpool, proj, skip, cot = operands
    count, wide = tokens.shape
    chans = qkv.shape[1]
    full = proj.shape[1]
    share_a = share_of(chans * (1 + full // wide), n)
    share_b = share_of(chans * 2, n)
    share_h = count // nh
    vmem = pl.BlockSpec(memory_space=pltpu.VMEM)
    outs = pl.pallas_call(
        functools.partial(kernel, n, nh, share_a, share_b),
        out_shape=(
            jax.ShapeDtypeStruct(cot.shape, BF16),
            jax.ShapeDtypeStruct(tokens.shape, BF16),
            jax.ShapeDtypeStruct(qkv.shape, BF16),
            jax.ShapeDtypeStruct(proj.shape, BF16),
        ),
        in_specs=[vmem] * 9,
        out_specs=(vmem,) * 4,
        scratch_shapes=[
            pltpu.VMEM((nh,) + cot.shape, BF16),
            pltpu.VMEM((2, n * SLAB, chans), BF16),
            pltpu.VMEM((2, n * SLAB, chans), BF16),
            pltpu.VMEM((2, n * SLAB, chans), BF16),
            pltpu.VMEM((2, CELLS // 2, wide), BF16),
            pltpu.VMEM((nh, CELLS // 2, wide), BF16),
            pltpu.VMEM((nh,) + cot.shape, BF16),
            pltpu.VMEM((nh,) + cot.shape, BF16),
            pltpu.VMEM((n * share_a, wide), BF16),
            pltpu.VMEM((n, share_a, wide), BF16),
            pltpu.VMEM((n * share_a, wide), BF16),
            pltpu.VMEM((n * share_b, wide), BF16),
            pltpu.VMEM((n, share_b, wide), BF16),
            pltpu.VMEM((n * share_b, wide), BF16),
            pltpu.VMEM((count, wide), BF16),
            pltpu.VMEM((nh, share_h, wide), BF16),
            pltpu.VMEM((count, wide), BF16),
            pltpu.VMEM((count, wide), F32),
            pltpu.VMEM((count, 128), F32),
            pltpu.SemaphoreType.DMA((6, n)),
            pltpu.SemaphoreType.DMA((6, n)),
            pltpu.SemaphoreType.DMA((5, nh)),
            pltpu.SemaphoreType.DMA((5, nh)),
        ],
        compiler_params=pltpu.CompilerParams(
            collective_id=0, has_side_effects=True, vmem_limit_bytes=40 * 1024 * 1024
        ),
    )(tokens, ln_gain.reshape(1, -1), qkv, qpool, kpool, vpool, proj, skip, cot)
    block_out, input_grad, qkv_grad, proj_grad = outs
    return (block_out, input_grad, qkv_grad.astype(F32), proj_grad.astype(F32))


def solution(mesh):
    placed = (
        P("tile", None),
        P(),
        P(None, "head", None),
        P(None, "head"),
        P(None, "head"),
        P(None, "head"),
        P("head", None),
        P("head", None),
        P("tile", "head"),
    )
    return jax.shard_map(
        functools.partial(local, mesh.shape["tile"], mesh.shape["head"]),
        mesh=mesh,
        in_specs=placed,
        out_specs=(P("tile", "head"), P("tile", None), P(None, "head", None), P("head", None)),
        check_vma=False,
    )
```

time: 217 us -> 41.8 us (0.19)
  waiting for transfers between devices: 119 us -> 0 us
  blocking collectives: 54.1 us -> 0 us
  Pallas kernels: 0 us -> 30.9 us
  between operations: 16.7 us -> 0.66 us
  matrix products: 7.79 us -> 0 us
  local copies, waits for them, and re-layouts: 13.6 us -> 7.94 us
  other arithmetic: 5.19 us -> 1.82 us
    psum x2 -> x0, waiting for transfers between devices: 91.1 us -> none  [the longest x1 59.9 us: local(): qkv_grad, proj_grad = lax.psum((qkv_part, proj_part), 'tile')]
    all_gather x3 -> x0, blocking collectives: 33.5 us -> none  [the longest x1 15 us: local(): full_cotangent = lax.all_gather(cotangent, 'head', axis=1, tiled=True)]
    pallas_call x0 -> x1, Pallas kernels: none -> 30.9 us  [local(): pl.pallas_call(functools.partial(kernel, n, nh, share_a, share_b), out_sh...]
    unnamed x6 -> x0, waiting for transfers between devices: 27.6 us -> none
    psum x1 -> x0, blocking collectives: 20.6 us -> none  [local(): lax.psum(d_pooled_part.astype(jnp.bfloat16), 'head').astype(jnp.float32)]
    dot_general x26 -> x0, matrix products: 7.79 us -> none  [the longest x1 1.08 us: local(): jnp.dot(attended.T, full_cotangent, preferred_element_type=jnp.float32)]
    reduce_sum x4 -> x0, other arithmetic: 2.79 us -> none  [the longest x1 1.24 us: norm_back(): jnp.mean(scaled, axis=-1, keepdims=True)]
    unnamed x30 -> x18, local copies, waits for them, and re-layouts: 9.38 us -> 7.25 us
  transfers between devices with their start and end apart: 4 -> 0, of which waited for: 3 -> 0; matrix products, arithmetic and copies ran while one was open for 6% -> 0% of each run, Pallas kernels for 0% -> 0%
where the time goes in v1:
time: 41.8 us; the launch traced here: 41.4 us
  Pallas kernels  30.9 us (74%)
  local copies, waits for them, and re-layouts  7.94 us (19%)
  other arithmetic  1.82 us (4%)
  between operations  0.66 us (2%)
    pallas_call x1, Pallas kernels, local(): pl.pallas_call(functools.partial(kernel, n, nh, share_a, share_b), out_sh...  30.9 us
    unnamed x18, local copies, waits for them, and re-layouts  7.25 us
    convert_element_type x2, other arithmetic, local(): return (block_out, input_grad, qkv_grad.astype(F32), proj_grad.astype(F32))  1.82 us

profile of v1, /device:TPU:0, one launch (start us, length us, event | category | flops | bytes accessed | tf_op | source)
XLA Modules:
  0.0 41.4 jit_solution(12426885368666935176)
XLA Ops:
  0.6 0.0 copy-start.7
  0.6 0.7 %reshape.11.gain_ref = f32[1,384]{1,0:T(1,128)S(1)} reshape(f32[384]{0:T(512)} %param.10) | data formatting | bytes 3072 | tf_op jit(solution)/shard_map/reshape | solution.py:455
  1.3 0.0 copy-done.7
  1.3 0.0 copy-start
  1.3 1.0 %copy-done = bf16[3,192,384]{2,1,0:T(8,128)(2,1)S(1)} copy-done((bf16[3,192,384]{2,1,0:T(8,128)(2,1)S(1)}, bf16[3,192,384]{2,1,0:T(8,128)(2,1)}, u32[]{:S(2)}) %copy-start) | copy-done | bytes 442392
  2.3 0.0 copy-start.1
  2.3 1.0 %copy-done.1 = bf16[192,768]{1,0:T(8,128)(2,1)S(1)} copy-done((bf16[192,768]{1,0:T(8,128)(2,1)S(1)}, bf16[192,768]{1,0:T(8,128)(2,1)}, u32[]{:S(2)}) %copy-start.1) | copy-done | bytes 294936
  3.3 0.0 copy-start.2
  3.3 0.9 %copy-done.2 = bf16[256,384]{1,0:T(8,128)(2,1)S(1)} copy-done((bf16[256,384]{1,0:T(8,128)(2,1)S(1)}, bf16[256,384]{1,0:T(8,128)(2,1)}, u32[]{:S(2)}) %copy-start.2) | copy-done | bytes 196632
  4.2 0.0 copy-start.3
  4.2 0.9 %copy-done.3 = bf16[192,384]{1,0:T(8,128)(2,1)S(1)} copy-done((bf16[192,384]{1,0:T(8,128)(2,1)S(1)}, bf16[192,384]{1,0:T(8,128)(2,1)}, u32[]{:S(2)}) %copy-start.3) | copy-done | bytes 147480
  5.1 0.0 copy-start.4
  5.1 0.8 %copy-done.4 = bf16[64,192]{1,0:T(8,128)(2,1)S(1)} copy-done((bf16[64,192]{1,0:T(8,128)(2,1)S(1)}, bf16[64,192]{1,0:T(8,128)(2,1)}, u32[]{:S(2)}) %copy-start.4) | copy-done | bytes 24600
  5.9 0.0 copy-start.5
  5.9 0.7 %copy-done.5 = bf16[16,192]{1,0:T(8,128)(2,1)S(1)} copy-done((bf16[16,192]{1,0:T(8,128)(2,1)S(1)}, bf16[16,192]{1,0:T(8,128)(2,1)}, u32[]{:S(2)}) %copy-start.5) | copy-done | bytes 6168
  6.6 0.0 copy-start.6
  6.6 0.7 %copy-done.6 = bf16[16,192]{1,0:T(8,128)(2,1)S(1)} copy-done((bf16[16,192]{1,0:T(8,128)(2,1)S(1)}, bf16[16,192]{1,0:T(8,128)(2,1)}, u32[]{:S(2)}) %copy-start.6) | copy-done | bytes 6168
  7.3 30.9 %shard_map.120 = (bf16[64,192]{1,0:T(8,128)(2,1)S(1)}, bf16[256,384]{1,0:T(8,128)(2,1)S(1)}, bf16[3,192,384]{2,1,0:T(8,128)(2,1)S(1)}, bf16[192,768]{1,0:T(8,128)(2,1)S(1)}) custom-call(bf16[256,384]{1,0:T(8,128)(2,1)S(1)} %copy-done.2, f32[1,384]{1,0:T(1,128)S(1)} %reshape.11.gain_ref, bf16[3,192,384]{2,1,0:T(8,128)(2,1)S(1)} %copy-done, ...), custom_call_target="tpu_custom_call" | custom-call | tf_op jit(solution)/shard_map/pallas_call | solution.py:417
  38.3 1.0 %convert_element_type.6 = f32[3,192,384]{2,1,0:T(8,128)} convert(bf16[3,192,384]{2,1,0:T(8,128)(2,1)S(1)} %get-tuple-element.10) | non-fusion elementwise | flops 221184 | bytes 1327104 | tf_op jit(solution)/shard_map/convert_element_type | solution.py:457
  39.2 0.9 %convert_element_type.7 = f32[192,768]{1,0:T(8,128)} convert(bf16[192,768]{1,0:T(8,128)(2,1)S(1)} %get-tuple-element.11) | non-fusion elementwise | flops 147456 | bytes 884736 | tf_op jit(solution)/shard_map/convert_element_type | solution.py:457
  40.1 0.6 %copy.15 = bf16[64,192]{1,0:T(8,128)(2,1)} copy(bf16[64,192]{1,0:T(8,128)(2,1)S(1)} %get-tuple-element.16) | data formatting | bytes 49152
  40.7 0.7 %copy.16 = bf16[256,384]{1,0:T(8,128)(2,1)} copy(bf16[256,384]{1,0:T(8,128)(2,1)S(1)} %get-tuple-element.17) | data formatting | bytes 393216
Async XLA Ops:
  0.6 0.7 %copy-start.7 = (bf16[4,192]{1,0:T(4,128)(2,1)S(1)}, bf16[4,192]{1,0:T(4,128)(2,1)}, u32[]{:S(2)}) copy-start(bf16[4,192]{1,0:T(4,128)(2,1)} %qpool_ref.1) | copy-start | bytes 4612
  1.3 1.0 %copy-start = (bf16[3,192,384]{2,1,0:T(8,128)(2,1)S(1)}, bf16[3,192,384]{2,1,0:T(8,128)(2,1)}, u32[]{:S(2)}) copy-start(bf16[3,192,384]{2,1,0:T(8,128)(2,1)} %qkv_ref.1) | copy-start | bytes 1327108
  2.3 1.0 %copy-start.1 = (bf16[192,768]{1,0:T(8,128)(2,1)S(1)}, bf16[192,768]{1,0:T(8,128)(2,1)}, u32[]{:S(2)}) copy-start(bf16[192,768]{1,0:T(8,128)(2,1)} %proj_ref.1) | copy-start | bytes 884740
  3.3 0.9 %copy-start.2 = (bf16[256,384]{1,0:T(8,128)(2,1)S(1)}, bf16[256,384]{1,0:T(8,128)(2,1)}, u32[]{:S(2)}) copy-start(bf16[256,384]{1,0:T(8,128)(2,1)} %tokens_ref.1) | copy-start | bytes 589828
  4.2 0.9 %copy-start.3 = (bf16[192,384]{1,0:T(8,128)(2,1)S(1)}, bf16[192,384]{1,0:T(8,128)(2,1)}, u32[]{:S(2)}) copy-start(bf16[192,384]{1,0:T(8,128)(2,1)} %skip_ref.1) | copy-start | bytes 442372
  5.1 0.8 %copy-start.4 = (bf16[64,192]{1,0:T(8,128)(2,1)S(1)}, bf16[64,192]{1,0:T(8,128)(2,1)}, u32[]{:S(2)}) copy-start(bf16[64,192]{1,0:T(8,128)(2,1)} %cot_ref.1) | copy-start | bytes 73732
  5.9 0.7 %copy-start.5 = (bf16[16,192]{1,0:T(8,128)(2,1)S(1)}, bf16[16,192]{1,0:T(8,128)(2,1)}, u32[]{:S(2)}) copy-start(bf16[16,192]{1,0:T(8,128)(2,1)} %kpool_ref.1) | copy-start | bytes 18436
  6.6 0.7 %copy-start.6 = (bf16[16,192]{1,0:T(8,128)(2,1)S(1)}, bf16[16,192]{1,0:T(8,128)(2,1)}, u32[]{:S(2)}) copy-start(bf16[16,192]{1,0:T(8,128)(2,1)} %vpool_ref.1) | copy-start | bytes 18436

commit v2 on v1

--- a/solution.py
+++ b/solution.py
@@ -54,6 +54,19 @@
     nh,
     share_a,
     share_b,
+    tokens_hbm,
+    gain_hbm,
+    qkv_hbm,
+    qpool_hbm,
+    kpool_hbm,
+    vpool_hbm,
+    proj_hbm,
+    skip_hbm,
+    cot_hbm,
+    block_out_ref,
+    ig_all,
+    ga_out,
+    gb_out,
     tokens_ref,
     gain_ref,
     qkv_ref,
@@ -63,10 +76,6 @@
     proj_ref,
     skip_ref,
     cot_ref,
-    block_out_ref,
-    input_grad_ref,
-    qkv_grad_ref,
-    proj_grad_ref,
     cot_all,
     kv_all,
     kvg_send,
@@ -76,16 +85,18 @@
     hp_send,
     hp_recv,
     ga_send,
+    ga_pair,
+    ga_part,
     ga_recv,
-    ga_out,
     gb_send,
+    gb_pair,
+    gb_part,
     gb_recv,
-    gb_out,
     dn_send,
     dn_recv,
-    ig_all,
     unit_ref,
     inv_ref,
+    load_sem,
     tile_send,
     tile_recv,
     head_send,
@@ -93,12 +104,19 @@
 ):
     me = lax.axis_index("tile")
     my_head = lax.axis_index("head")
+    chips = n // 2
+    chip, core = me // 2, lax.rem(me, 2)
     chans = qkv_ref.shape[1]
     wide = qkv_ref.shape[2]
     share_h = unit_ref.shape[0] // nh
 
     def at_tile(k):
         return (lax.rem(me + k, n), my_head)
+
+    def at_chip(k):
+        return (lax.rem(chip + k, chips) * 2 + core, my_head)
+
+    partner = (chip * 2 + 1 - core, my_head)
 
     def at_head(k):
         return (me, lax.rem(my_head + k, nh))
@@ -140,16 +158,37 @@
     for k in range(1, nh):
         pl.semaphore_signal(barrier, inc=1, device_id=at_head(k), device_id_type=MESH)
 
+    loads = {}
+    for i, (name, src, dst) in enumerate(
+        (
+            ("tokens", tokens_hbm, tokens_ref),
+            ("gain", gain_hbm, gain_ref),
+            ("qkv", qkv_hbm, qkv_ref),
+            ("kpool", kpool_hbm, kpool_ref),
+            ("vpool", vpool_hbm, vpool_ref),
+            ("cot", cot_hbm, cot_ref),
+            ("qpool", qpool_hbm, qpool_ref),
+            ("skip", skip_hbm, skip_ref),
+            ("proj", proj_hbm, proj_ref),
+        )
+    ):
+        loads[name] = pltpu.make_async_copy(src, dst, load_sem.at[i])
+        loads[name].start()
+
     order = one_hot(token_order, TILE_H * TILE_W)
+    loads["tokens"].wait()
     tokens = mm(order, tokens_ref[...])
     center = tokens - jnp.mean(tokens, axis=-1, keepdims=True)
     inv_std = lax.rsqrt(jnp.mean(center * center, axis=-1, keepdims=True) + EPSILON)
     unit = center * inv_std
     unit_ref[...] = unit
     inv_ref[...] = jnp.broadcast_to(inv_std, inv_ref.shape)
-    gain = gain_ref[...]
+    loads["gain"].wait()
+    gain = gain_ref[...].reshape(1, wide)
     normed = (unit * gain).astype(BF16)
 
+    for name in ("qkv", "kpool", "vpool", "cot", "qpool"):
+        loads[name].wait()
     kpool = kpool_ref[...].astype(F32)
     vpool = vpool_ref[...].astype(F32)
     qpool = qpool_ref[...].astype(F32)
@@ -204,6 +243,7 @@
     cells = one_hot(cell_order, CELLS)
     cells_back = one_hot(cell_order, CELLS, transposed=True)
     pooled_input = mm(cells_back, pooled_input).astype(BF16)
+    loads["skip"].wait()
     skipped = mm(pooled_input, skip_ref[...], (1, 1))
 
     own_cot = mm(cells, cot_ref[...]).astype(BF16)
@@ -222,6 +262,7 @@
         for k in range(1, nh)
     ]
 
+    loads["proj"].wait()
     arrived(cot_copies)
     full_cot = jnp.concatenate([cot_all[h] for h in range(nh)], axis=1)
     full_cot = mm(cells, full_cot).astype(BF16)
@@ -296,40 +337,21 @@
     filled = (halves + 1) * chans
     if ga_send.shape[0] > filled:
         ga_send[filled:, :] = jnp.zeros((ga_send.shape[0] - filled, wide), BF16)
-    ga_copies = [
-        send_tile(
-            2,
-            k,
-            ga_send.at[rows(lax.rem(me + k, n) * share_a, share_a)],
-            ga_recv.at[k],
-            at_tile(k),
-        )
-        for k in range(1, n)
+    half_a, half_b = chips * share_a, chips * share_b
+    ga_pairs = [
+        send_tile(2, 1, ga_send.at[rows((1 - core) * half_a, half_a)], ga_pair, partner)
     ]
     d_normed = mm(d_projected, qkv_ref[0])
 
     arrived(kvg_copies)
+    d_fields = []
     for j, pool, own in ((0, kpool, key_grad), (1, vpool, value_grad)):
         total = own[0:SLAB]
         for k in range(1, n):
             total = total + kvg_recv[j, k * SLAB : (k + 1) * SLAB, :].astype(F32)
         d_projected = jnp.concatenate([pool[s : s + 1] * total for s in range(16)], axis=0)
-        d_projected = d_projected.astype(BF16)
-        gb_send[j * chans : (j + 1) * chans, :] = mm(d_projected, normed, (0, 0)).astype(BF16)
-        d_normed = d_normed + mm(d_projected, qkv_ref[j + 1])
-    filled = 2 * chans
-    if gb_send.shape[0] > filled:
-        gb_send[filled:, :] = jnp.zeros((gb_send.shape[0] - filled, wide), BF16)
-    gb_copies = [
-        send_tile(
-            3,
-            k,
-            gb_send.at[rows(lax.rem(me + k, n) * share_b, share_b)],
-            gb_recv.at[k],
-            at_tile(k),
-        )
-        for k in range(1, n)
-    ]
+        d_fields.append(d_projected.astype(BF16))
+        d_normed = d_normed + mm(d_fields[j], qkv_ref[j + 1])
     dn_send[...] = d_normed.astype(BF16)
     dn_copies = [
         send_head(
@@ -341,19 +363,58 @@
         )
         for k in range(1, nh)
     ]
-
-    def reduce_and_share(stage, copies, sent, received, out, share):
+    for j in range(2):
+        gb_send[j * chans : (j + 1) * chans, :] = mm(d_fields[j], normed, (0, 0)).astype(BF16)
+    filled = 2 * chans
+    if gb_send.shape[0] > filled:
+        gb_send[filled:, :] = jnp.zeros((gb_send.shape[0] - filled, wide), BF16)
+    gb_pairs = [
+        send_tile(6, 1, gb_send.at[rows((1 - core) * half_b, half_b)], gb_pair, partner)
+    ]
+
+    def fold(stage, pairs, sent, pair, part, received, share):
+        arrived(pairs)
+        size = chips * share
+        total = sent[rows(core * size, size), :].astype(F32) + pair[...].astype(F32)
+        part[...] = total.astype(BF16)
+        return [
+            send_tile(
+                stage,
+                k,
+                part.at[rows(lax.rem(chip + k, chips) * share, share)],
+                received.at[k],
+                at_chip(k),
+            )
+            for k in range(1, chips)
+        ]
+
+    def place(k, share):
+        from_chip = lax.rem(chip + chips - k, chips)
+        return rows((core * chips + from_chip) * share, share)
+
+    def reduce_and_share(stage, copies, part, received, out, share):
         arrived(copies)
-        mine = rows(me * share, share)
-        total = sent[mine, :].astype(F32)
-        for k in range(1, n):
+        total = part[rows(chip * share, share), :].astype(F32)
+        for k in range(1, chips):
             total = total + received[k].astype(F32)
+        mine = place(0, share)
         out[mine, :] = total.astype(BF16)
-        return [
-            send_tile(stage, k, out.at[mine], out.at[mine], at_tile(k)) for k in range(1, n)
+        shares = [
+            send_tile(stage, k, out.at[mine], out.at[mine], at_chip(k))
+            for k in range(1, chips)
         ]
-
-    ga_copies = reduce_and_share(4, ga_copies, ga_send, ga_recv, ga_out, share_a)
+        relays = [send_tile(stage + 1, 0, out.at[mine], out.at[mine], partner)]
+        return shares, relays
+
+    def relay(stage, shares, relays, out, share):
+        for k in range(1, chips):
+            arrived(shares[k - 1 : k])
+            there = place(k, share)
+            relays.append(send_tile(stage, k, out.at[there], out.at[there], partner))
+
+    ga_copies = fold(3, ga_pairs, ga_send, ga_pair, ga_part, ga_recv, share_a)
+    gb_copies = fold(7, gb_pairs, gb_send, gb_pair, gb_part, gb_recv, share_b)
+    ga_shares, ga_relays = reduce_and_share(4, ga_copies, ga_part, ga_recv, ga_out, share_a)
 
     arrived(hp_copies)
     summed = hp_send[my_head].astype(F32)
@@ -384,21 +445,43 @@
         send_head(4, k, ig_all.at[mine], ig_all.at[mine], at_head(k)) for k in range(1, nh)
     ]
 
-    gb_copies = reduce_and_share(5, gb_copies, gb_send, gb_recv, gb_out, share_b)
-
-    arrived(ga_copies)
-    qkv_grad_ref[0] = ga_out[0:chans, :]
-    for i in range(halves):
-        proj_grad_ref[:, i * wide : (i + 1) * wide] = ga_out[(i + 1) * chans : (i + 2) * chans, :]
+    gb_shares, gb_relays = reduce_and_share(8, gb_copies, gb_part, gb_recv, gb_out, share_b)
+    relay(5, ga_shares, ga_relays, ga_out, share_a)
+    relay(9, gb_shares, gb_relays, gb_out, share_b)
     arrived(ig_copies)
-    input_grad_ref[...] = mm(
-        one_hot(token_order, TILE_H * TILE_W, transposed=True), ig_all[...]
-    ).astype(BF16)
-    arrived(gb_copies)
-    qkv_grad_ref[1] = gb_out[0:chans, :]
-    qkv_grad_ref[2] = gb_out[chans : 2 * chans, :]
+    arrived(ga_relays)
+    arrived(gb_relays)
     for copy in started:
         copy.wait_send()
+
+
+def finish(
+    block_ref, ig_ref, ga_ref, gb_ref, block_hbm, ig_hbm, qkv_hbm, proj_hbm, ig, qkv, proj, sems
+):
+    chans, wide = qkv.shape[1:]
+    copies = [pltpu.make_async_copy(block_ref, block_hbm, sems.at[0])]
+    copies[0].start()
+
+    def put(src, dst):
+        copy = pltpu.make_async_copy(src, dst, sems.at[len(copies)])
+        copy.start()
+        copies.append(copy)
+
+    for i in range(proj.shape[1] // wide):
+        proj[:, i * wide : (i + 1) * wide] = ga_ref[
+            (i + 1) * chans : (i + 2) * chans, :
+        ].astype(F32)
+    put(proj, proj_hbm)
+    for j, part in enumerate(
+        (ga_ref[0:chans, :], gb_ref[0:chans, :], gb_ref[chans : 2 * chans, :])
+    ):
+        qkv[j] = part.astype(F32)
+        put(qkv.at[j], qkv_hbm.at[j])
+    back = one_hot(token_order, TILE_H * TILE_W, transposed=True)
+    ig[...] = mm(back, ig_ref[...]).astype(BF16)
+    put(ig, ig_hbm)
+    for copy in copies:
+        copy.wait()
 
 
 def share_of(total, n):
@@ -414,17 +497,19 @@
     share_b = share_of(chans * 2, n)
     share_h = count // nh
     vmem = pl.BlockSpec(memory_space=pltpu.VMEM)
+    hbm = pl.BlockSpec(memory_space=pltpu.HBM)
     outs = pl.pallas_call(
         functools.partial(kernel, n, nh, share_a, share_b),
         out_shape=(
             jax.ShapeDtypeStruct(cot.shape, BF16),
             jax.ShapeDtypeStruct(tokens.shape, BF16),
-            jax.ShapeDtypeStruct(qkv.shape, BF16),
-            jax.ShapeDtypeStruct(proj.shape, BF16),
+            jax.ShapeDtypeStruct((n * share_a, wide), BF16),
+            jax.ShapeDtypeStruct((n * share_b, wide), BF16),
         ),
-        in_specs=[vmem] * 9,
+        in_specs=[hbm] * 9,
         out_specs=(vmem,) * 4,
-        scratch_shapes=[
+        scratch_shapes=[pltpu.VMEM(x.shape, x.dtype) for x in operands]
+        + [
             pltpu.VMEM((nh,) + cot.shape, BF16),
             pltpu.VMEM((2, n * SLAB, chans), BF16),
             pltpu.VMEM((2, n * SLAB, chans), BF16),
@@ -434,27 +519,45 @@
             pltpu.VMEM((nh,) + cot.shape, BF16),
             pltpu.VMEM((nh,) + cot.shape, BF16),
             pltpu.VMEM((n * share_a, wide), BF16),
-            pltpu.VMEM((n, share_a, wide), BF16),
-            pltpu.VMEM((n * share_a, wide), BF16),
+            pltpu.VMEM((n // 2 * share_a, wide), BF16),
+            pltpu.VMEM((n // 2 * share_a, wide), BF16),
+            pltpu.VMEM((n // 2, share_a, wide), BF16),
             pltpu.VMEM((n * share_b, wide), BF16),
-            pltpu.VMEM((n, share_b, wide), BF16),
-            pltpu.VMEM((n * share_b, wide), BF16),
+            pltpu.VMEM((n // 2 * share_b, wide), BF16),
+            pltpu.VMEM((n // 2 * share_b, wide), BF16),
+            pltpu.VMEM((n // 2, share_b, wide), BF16),
             pltpu.VMEM((count, wide), BF16),
             pltpu.VMEM((nh, share_h, wide), BF16),
-            pltpu.VMEM((count, wide), BF16),
             pltpu.VMEM((count, wide), F32),
             pltpu.VMEM((count, 128), F32),
-            pltpu.SemaphoreType.DMA((6, n)),
-            pltpu.SemaphoreType.DMA((6, n)),
+            pltpu.SemaphoreType.DMA((9,)),
+            pltpu.SemaphoreType.DMA((10, n)),
+            pltpu.SemaphoreType.DMA((10, n)),
             pltpu.SemaphoreType.DMA((5, nh)),
             pltpu.SemaphoreType.DMA((5, nh)),
         ],
         compiler_params=pltpu.CompilerParams(
             collective_id=0, has_side_effects=True, vmem_limit_bytes=40 * 1024 * 1024
         ),
-    )(tokens, ln_gain.reshape(1, -1), qkv, qpool, kpool, vpool, proj, skip, cot)
-    block_out, input_grad, qkv_grad, proj_grad = outs
-    return (block_out, input_grad, qkv_grad.astype(F32), proj_grad.astype(F32))
+    )(*[pltpu.with_memory_space_constraint(x, pltpu.HBM) for x in operands])
+    return pl.pallas_call(
+        finish,
+        out_shape=(
+            jax.ShapeDtypeStruct(cot.shape, BF16),
+            jax.ShapeDtypeStruct(tokens.shape, BF16),
+            jax.ShapeDtypeStruct(qkv.shape, F32),
+            jax.ShapeDtypeStruct(proj.shape, F32),
+        ),
+        in_specs=[vmem] * 4,
+        out_specs=(hbm,) * 4,
+        scratch_shapes=[
+            pltpu.VMEM(tokens.shape, BF16),
+            pltpu.VMEM(qkv.shape, F32),
+            pltpu.VMEM(proj.shape, F32),
+            pltpu.SemaphoreType.DMA((6,)),
+        ],
+        compiler_params=pltpu.CompilerParams(vmem_limit_bytes=16 * 1024 * 1024),
+    )(*outs)
 
 
 def solution(mesh):

time: 41.8 us -> 31.5 us (0.75)
  local copies, waits for them, and re-layouts: 7.94 us -> 0 us
  other arithmetic: 1.82 us -> 0 us
    unnamed x18 -> x0, local copies, waits for them, and re-layouts: 7.25 us -> none
    convert_element_type x2 -> x0, other arithmetic: 1.82 us -> none  [local(): return (block_out, input_grad, qkv_grad.astype(F32), proj_grad.astype(F32))]
    pallas_call x1, Pallas kernels: 30.9 us -> 29.3 us  [local(): pl.pallas_call(functools.partial(kernel, n, nh, share_a, share_b), out_sh...]
    pallas_call x0 -> x1, Pallas kernels: none -> 1.39 us  [local(): pl.pallas_call(finish, out_shape=(jax.ShapeDtypeStruct(cot.shape, BF16),...]
    reshape x1 -> x0, local copies, waits for them, and re-layouts: 0.69 us -> none  [local(): ln_gain.reshape(1, -1)]
where the time goes in v2:
time: 31.5 us; the launch traced here: 31.3 us
  Pallas kernels  30.7 us (97%)
  between operations  0.64 us (2%)
    pallas_call x1, Pallas kernels, local(): pl.pallas_call(functools.partial(kernel, n, nh, share_a, share_b), out_sh...  29.3 us
    pallas_call x1, Pallas kernels, local(): pl.pallas_call(finish, out_shape=(jax.ShapeDtypeStruct(cot.shape, BF16),...  1.39 us

profile of v2, /device:TPU:0, one launch (start us, length us, event | category | flops | bytes accessed | tf_op | source)
XLA Modules:
  0.0 31.3 jit_solution(16579092705081992505)
XLA Ops:
  0.6 29.3 %shard_map.120 = (bf16[64,192]{1,0:T(8,128)(2,1)S(1)}, bf16[256,384]{1,0:T(8,128)(2,1)S(1)}, bf16[640,384]{1,0:T(8,128)(2,1)S(1)}, bf16[384,384]{1,0:T(8,128)(2,1)S(1)}) custom-call(bf16[256,384]{1,0:T(8,128)(2,1)} %tokens_hbm.1, f32[384]{0:T(512)} %gain_hbm.1, bf16[3,192,384]{2,1,0:T(8,128)(2,1)} %qkv_hbm.1, bf16[4,192]{1,0:T(4,128)(2,1)} %qpool_hbm.1, ...), custom_call_target="tpu_custom_call" | custom-call | tf_op jit(solution)/shard_map/pallas_call | solution.py:501
  29.9 1.4 %shard_map.121 = (bf16[64,192]{1,0:T(8,128)(2,1)}, bf16[256,384]{1,0:T(8,128)(2,1)}, f32[3,192,384]{2,1,0:T(8,128)}, f32[192,768]{1,0:T(8,128)}) custom-call(bf16[64,192]{1,0:T(8,128)(2,1)S(1)} %get-tuple-element.8.block_ref, bf16[256,384]{1,0:T(8,128)(2,1)S(1)} %get-tuple-element.9.ig_ref, bf16[640,384]{1,0:T(8,128)(2,1)S(1)} %get-tuple-element.10.ga_ref, ...), custom_call_target="tpu_custom_call" | custom-call | tf_op jit(solution)/shard_map/pallas_call | solution.py:543

commit v3 on v2

--- a/solution.py
+++ b/solution.py
@@ -161,12 +161,12 @@
     loads = {}
     for i, (name, src, dst) in enumerate(
         (
+            ("cot", cot_hbm, cot_ref),
             ("tokens", tokens_hbm, tokens_ref),
             ("gain", gain_hbm, gain_ref),
             ("qkv", qkv_hbm, qkv_ref),
             ("kpool", kpool_hbm, kpool_ref),
             ("vpool", vpool_hbm, vpool_ref),
-            ("cot", cot_hbm, cot_ref),
             ("qpool", qpool_hbm, qpool_ref),
             ("skip", skip_hbm, skip_ref),
             ("proj", proj_hbm, proj_ref),
@@ -174,6 +174,13 @@
     ):
         loads[name] = pltpu.make_async_copy(src, dst, load_sem.at[i])
         loads[name].start()
+
+    loads["cot"].wait()
+    cot_all[my_head] = cot_ref[...]
+    pl.semaphore_wait(barrier, n + nh - 2)
+    cot_copies = [
+        send_head(0, k, cot_ref, cot_all.at[my_head], at_head(k)) for k in range(1, nh)
+    ]
 
     order = one_hot(token_order, TILE_H * TILE_W)
     loads["tokens"].wait()
@@ -187,11 +194,10 @@
     gain = gain_ref[...].reshape(1, wide)
     normed = (unit * gain).astype(BF16)
 
-    for name in ("qkv", "kpool", "vpool", "cot", "qpool"):
+    for name in ("qkv", "kpool", "vpool"):
         loads[name].wait()
     kpool = kpool_ref[...].astype(F32)
     vpool = vpool_ref[...].astype(F32)
-    qpool = qpool_ref[...].astype(F32)
 
     def pool_block(field, pool):
         total = pool[0:1] * field[0:SLAB]
@@ -202,7 +208,6 @@
     kv_all[0, 0:SLAB, :] = pool_block(mm(normed, qkv_ref[1], (1, 1)), kpool).astype(BF16)
     kv_all[1, 0:SLAB, :] = pool_block(mm(normed, qkv_ref[2], (1, 1)), vpool).astype(BF16)
 
-    pl.semaphore_wait(barrier, n + nh - 2)
     kv_copies = [
         send_tile(
             0,
@@ -213,16 +218,14 @@
         )
         for k in range(1, n)
     ]
-    cot_copies = [
-        send_head(0, k, cot_ref, cot_all.at[my_head], at_head(k)) for k in range(1, nh)
-    ]
-    cot_all[my_head] = cot_ref[...]
 
     def cell_slabs(a, b):
         return [
             (2 * a2 + b2, (2 * a + a2) * 4 + 2 * b + b2) for a2 in range(2) for b2 in range(2)
         ]
 
+    loads["qpool"].wait()
+    qpool = qpool_ref[...].astype(F32)
     field = mm(normed, qkv_ref[0], (1, 1))
     query_parts = []
     input_parts = []
@@ -242,9 +245,7 @@
 
     cells = one_hot(cell_order, CELLS)
     cells_back = one_hot(cell_order, CELLS, transposed=True)
-    pooled_input = mm(cells_back, pooled_input).astype(BF16)
     loads["skip"].wait()
-    skipped = mm(pooled_input, skip_ref[...], (1, 1))
 
     own_cot = mm(cells, cot_ref[...]).astype(BF16)
     d_pooled = mm(own_cot, skip_ref[...]).astype(BF16)
@@ -343,6 +344,48 @@
     ]
     d_normed = mm(d_projected, qkv_ref[0])
 
+    def fold(stage, pairs, sent, pair, part, received, share):
+        arrived(pairs)
+        size = chips * share
+        total = sent[rows(core * size, size), :].astype(F32) + pair[...].astype(F32)
+        part[...] = total.astype(BF16)
+        return [
+            send_tile(
+                stage,
+                k,
+                part.at[rows(lax.rem(chip + k, chips) * share, share)],
+                received.at[k],
+                at_chip(k),
+            )
+            for k in range(1, chips)
+        ]
+
+    def place(k, share):
+        from_chip = lax.rem(chip + chips - k, chips)
+        return rows((core * chips + from_chip) * share, share)
+
+    def reduce_and_share(stage, copies, part, received, out, share):
+        arrived(copies)
+        total = part[rows(chip * share, share), :].astype(F32)
+        for k in range(1, chips):
+            total = total + received[k].astype(F32)
+        mine = place(0, share)
+        out[mine, :] = total.astype(BF16)
+        shares = [
+            send_tile(stage, k, out.at[mine], out.at[mine], at_chip(k))
+            for k in range(1, chips)
+        ]
+        relays = [send_tile(stage + 1, 0, out.at[mine], out.at[mine], partner)]
+        return shares, relays
+
+    def relay(stage, shares, relays, out, share):
+        for k in range(1, chips):
+            arrived(shares[k - 1 : k])
+            there = place(k, share)
+            relays.append(send_tile(stage, k, out.at[there], out.at[there], partner))
+
+    ga_copies = fold(3, ga_pairs, ga_send, ga_pair, ga_part, ga_recv, share_a)
+
     arrived(kvg_copies)
     d_fields = []
     for j, pool, own in ((0, kpool, key_grad), (1, vpool, value_grad)):
@@ -372,50 +415,11 @@
         send_tile(6, 1, gb_send.at[rows((1 - core) * half_b, half_b)], gb_pair, partner)
     ]
 
-    def fold(stage, pairs, sent, pair, part, received, share):
-        arrived(pairs)
-        size = chips * share
-        total = sent[rows(core * size, size), :].astype(F32) + pair[...].astype(F32)
-        part[...] = total.astype(BF16)
-        return [
-            send_tile(
-                stage,
-                k,
-                part.at[rows(lax.rem(chip + k, chips) * share, share)],
-                received.at[k],
-                at_chip(k),
-            )
-            for k in range(1, chips)
-        ]
-
-    def place(k, share):
-        from_chip = lax.rem(chip + chips - k, chips)
-        return rows((core * chips + from_chip) * share, share)
-
-    def reduce_and_share(stage, copies, part, received, out, share):
-        arrived(copies)
-        total = part[rows(chip * share, share), :].astype(F32)
-        for k in range(1, chips):
-            total = total + received[k].astype(F32)
-        mine = place(0, share)
-        out[mine, :] = total.astype(BF16)
-        shares = [
-            send_tile(stage, k, out.at[mine], out.at[mine], at_chip(k))
-            for k in range(1, chips)
-        ]
-        relays = [send_tile(stage + 1, 0, out.at[mine], out.at[mine], partner)]
-        return shares, relays
-
-    def relay(stage, shares, relays, out, share):
-        for k in range(1, chips):
-            arrived(shares[k - 1 : k])
-            there = place(k, share)
-            relays.append(send_tile(stage, k, out.at[there], out.at[there], partner))
-
-    ga_copies = fold(3, ga_pairs, ga_send, ga_pair, ga_part, ga_recv, share_a)
     gb_copies = fold(7, gb_pairs, gb_send, gb_pair, gb_part, gb_recv, share_b)
     ga_shares, ga_relays = reduce_and_share(4, ga_copies, ga_part, ga_recv, ga_out, share_a)
 
+    pooled_input = mm(cells_back, pooled_input).astype(BF16)
+    skipped = mm(pooled_input, skip_ref[...], (1, 1))
     arrived(hp_copies)
     summed = hp_send[my_head].astype(F32)
     for k in range(1, nh):
@@ -459,14 +463,17 @@
     block_ref, ig_ref, ga_ref, gb_ref, block_hbm, ig_hbm, qkv_hbm, proj_hbm, ig, qkv, proj, sems
 ):
     chans, wide = qkv.shape[1:]
-    copies = [pltpu.make_async_copy(block_ref, block_hbm, sems.at[0])]
-    copies[0].start()
+    copies = []
 
     def put(src, dst):
         copy = pltpu.make_async_copy(src, dst, sems.at[len(copies)])
         copy.start()
         copies.append(copy)
 
+    back = one_hot(token_order, TILE_H * TILE_W, transposed=True)
+    ig[...] = mm(back, ig_ref[...]).astype(BF16)
+    put(ig, ig_hbm)
+    put(block_ref, block_hbm)
     for i in range(proj.shape[1] // wide):
         proj[:, i * wide : (i + 1) * wide] = ga_ref[
             (i + 1) * chans : (i + 2) * chans, :
@@ -477,9 +484,6 @@
     ):
         qkv[j] = part.astype(F32)
         put(qkv.at[j], qkv_hbm.at[j])
-    back = one_hot(token_order, TILE_H * TILE_W, transposed=True)
-    ig[...] = mm(back, ig_ref[...]).astype(BF16)
-    put(ig, ig_hbm)
     for copy in copies:
         copy.wait()
 

time: 31.5 us -> 31.9 us (1.013)
  Pallas kernels: 30.7 us -> 31.1 us
    pallas_call x1, Pallas kernels: 29.3 us -> 29.7 us  [local(): pl.pallas_call(functools.partial(kernel, n, nh, share_a, share_b), out_sh...]
where the time goes in v3:
time: 31.9 us; the launch traced here: 31.8 us
  Pallas kernels  31.1 us (97%)
  between operations  0.64 us (2%)
    pallas_call x1, Pallas kernels, local(): pl.pallas_call(functools.partial(kernel, n, nh, share_a, share_b), out_sh...  29.7 us
    pallas_call x1, Pallas kernels, local(): pl.pallas_call(finish, out_shape=(jax.ShapeDtypeStruct(cot.shape, BF16),...  1.45 us

profile of v3, /device:TPU:0, one launch (start us, length us, event | category | flops | bytes accessed | tf_op | source)
XLA Modules:
  0.0 31.8 jit_solution(1436866589083141599)
XLA Ops:
  0.6 29.7 %shard_map.120 = (bf16[64,192]{1,0:T(8,128)(2,1)S(1)}, bf16[256,384]{1,0:T(8,128)(2,1)S(1)}, bf16[640,384]{1,0:T(8,128)(2,1)S(1)}, bf16[384,384]{1,0:T(8,128)(2,1)S(1)}) custom-call(bf16[256,384]{1,0:T(8,128)(2,1)} %tokens_hbm.1, f32[384]{0:T(512)} %gain_hbm.1, bf16[3,192,384]{2,1,0:T(8,128)(2,1)} %qkv_hbm.1, bf16[4,192]{1,0:T(4,128)(2,1)} %qpool_hbm.1, ...), custom_call_target="tpu_custom_call" | custom-call | tf_op jit(solution)/shard_map/pallas_call | solution.py:505
  30.3 1.5 %shard_map.121 = (bf16[64,192]{1,0:T(8,128)(2,1)}, bf16[256,384]{1,0:T(8,128)(2,1)}, f32[3,192,384]{2,1,0:T(8,128)}, f32[192,768]{1,0:T(8,128)}) custom-call(bf16[64,192]{1,0:T(8,128)(2,1)S(1)} %get-tuple-element.8.block_ref, bf16[256,384]{1,0:T(8,128)(2,1)S(1)} %get-tuple-element.9.ig_ref, bf16[640,384]{1,0:T(8,128)(2,1)S(1)} %get-tuple-element.10.ga_ref, ...), custom_call_target="tpu_custom_call" | custom-call | tf_op jit(solution)/shard_map/pallas_call | solution.py:547

commit v4 on v3

--- a/solution.py
+++ b/solution.py
@@ -396,15 +396,19 @@
         d_fields.append(d_projected.astype(BF16))
         d_normed = d_normed + mm(d_fields[j], qkv_ref[j + 1])
     dn_send[...] = d_normed.astype(BF16)
+    piece = share_h // 2
     dn_copies = [
-        send_head(
-            3,
-            k,
-            dn_send.at[rows(lax.rem(my_head + k, nh) * share_h, share_h)],
-            dn_recv.at[k],
-            at_head(k),
-        )
-        for k in range(1, nh)
+        [
+            send_head(
+                3 + half,
+                k,
+                dn_send.at[rows(lax.rem(my_head + k, nh) * share_h + half * piece, piece)],
+                dn_recv.at[k, half * piece : (half + 1) * piece],
+                at_head(k),
+            )
+            for k in range(1, nh)
+        ]
+        for half in range(2)
     ]
     for j in range(2):
         gb_send[j * chans : (j + 1) * chans, :] = mm(d_fields[j], normed, (0, 0)).astype(BF16)
@@ -430,26 +434,31 @@
     d_pooled = dp_send[my_head * 2 // nh].astype(F32)
     for k in range(1, nh):
         d_pooled = d_pooled + dp_recv[k].astype(F32)
-    arrived(dn_copies)
-    mine = rows(my_head * share_h, share_h)
-    d_normed = dn_send[mine, :].astype(F32)
-    for k in range(1, nh):
-        d_normed = d_normed + dn_recv[k].astype(F32)
-    scaled = d_normed * gain
-    own_unit = unit_ref[mine, :]
-    back = inv_ref[mine, :][:, 0:1] * (
-        scaled
-        - jnp.mean(scaled, axis=-1, keepdims=True)
-        - own_unit * jnp.mean(scaled * own_unit, axis=-1, keepdims=True)
-    )
-    left, right = d_pooled[:SLAB], d_pooled[SLAB:]
-    back = back + jnp.concatenate([left, left, right, right], axis=0) * 0.25
-    ig_all[mine, :] = back.astype(BF16)
-    ig_copies = [
-        send_head(4, k, ig_all.at[mine], ig_all.at[mine], at_head(k)) for k in range(1, nh)
-    ]
-
+    d_pooled = d_pooled * 0.25
+
+    def share_input(half):
+        arrived(dn_copies[half])
+        mine = rows(my_head * share_h + half * piece, piece)
+        d_normed = dn_send[mine, :].astype(F32)
+        for k in range(1, nh):
+            d_normed = d_normed + dn_recv[k, half * piece : (half + 1) * piece, :].astype(F32)
+        scaled = d_normed * gain
+        own_unit = unit_ref[mine, :]
+        back = inv_ref[mine, :][:, 0:1] * (
+            scaled
+            - jnp.mean(scaled, axis=-1, keepdims=True)
+            - own_unit * jnp.mean(scaled * own_unit, axis=-1, keepdims=True)
+        )
+        cell = d_pooled[half * SLAB : (half + 1) * SLAB]
+        ig_all[mine, :] = (back + jnp.concatenate([cell, cell], axis=0)).astype(BF16)
+        return [
+            send_head(5 + half, k, ig_all.at[mine], ig_all.at[mine], at_head(k))
+            for k in range(1, nh)
+        ]
+
+    ig_copies = share_input(0)
     gb_shares, gb_relays = reduce_and_share(8, gb_copies, gb_part, gb_recv, gb_out, share_b)
+    ig_copies += share_input(1)
     relay(5, ga_shares, ga_relays, ga_out, share_a)
     relay(9, gb_shares, gb_relays, gb_out, share_b)
     arrived(ig_copies)
@@ -537,8 +546,8 @@
             pltpu.SemaphoreType.DMA((9,)),
             pltpu.SemaphoreType.DMA((10, n)),
             pltpu.SemaphoreType.DMA((10, n)),
-            pltpu.SemaphoreType.DMA((5, nh)),
-            pltpu.SemaphoreType.DMA((5, nh)),
+            pltpu.SemaphoreType.DMA((7, nh)),
+            pltpu.SemaphoreType.DMA((7, nh)),
         ],
         compiler_params=pltpu.CompilerParams(
             collective_id=0, has_side_effects=True, vmem_limit_bytes=40 * 1024 * 1024

time: 31.9 us -> 31.3 us (0.981)
  Pallas kernels: 31.1 us -> 30.5 us
    pallas_call x1, Pallas kernels: 29.7 us -> 29.1 us  [local(): pl.pallas_call(functools.partial(kernel, n, nh, share_a, share_b), out_sh...]
where the time goes in v4:
time: 31.3 us; the launch traced here: 31.2 us
  Pallas kernels  30.5 us (97%)
  between operations  0.64 us (2%)
    pallas_call x1, Pallas kernels, local(): pl.pallas_call(functools.partial(kernel, n, nh, share_a, share_b), out_sh...  29.1 us
    pallas_call x1, Pallas kernels, local(): pl.pallas_call(finish, out_shape=(jax.ShapeDtypeStruct(cot.shape, BF16),...  1.45 us

profile of v4, /device:TPU:0, one launch (start us, length us, event | category | flops | bytes accessed | tf_op | source)
XLA Modules:
  0.0 31.2 jit_solution(4981691708595658707)
XLA Ops:
  0.6 29.1 %shard_map.120 = (bf16[64,192]{1,0:T(8,128)(2,1)S(1)}, bf16[256,384]{1,0:T(8,128)(2,1)S(1)}, bf16[640,384]{1,0:T(8,128)(2,1)S(1)}, bf16[384,384]{1,0:T(8,128)(2,1)S(1)}) custom-call(bf16[256,384]{1,0:T(8,128)(2,1)} %tokens_hbm.1, f32[384]{0:T(512)} %gain_hbm.1, bf16[3,192,384]{2,1,0:T(8,128)(2,1)} %qkv_hbm.1, bf16[4,192]{1,0:T(4,128)(2,1)} %qpool_hbm.1, ...), custom_call_target="tpu_custom_call" | custom-call | tf_op jit(solution)/shard_map/pallas_call | solution.py:514
  29.7 1.5 %shard_map.121 = (bf16[64,192]{1,0:T(8,128)(2,1)}, bf16[256,384]{1,0:T(8,128)(2,1)}, f32[3,192,384]{2,1,0:T(8,128)}, f32[192,768]{1,0:T(8,128)}) custom-call(bf16[64,192]{1,0:T(8,128)(2,1)S(1)} %get-tuple-element.8.block_ref, bf16[256,384]{1,0:T(8,128)(2,1)S(1)} %get-tuple-element.9.ig_ref, bf16[640,384]{1,0:T(8,128)(2,1)S(1)} %get-tuple-element.10.ga_ref, ...), custom_call_target="tpu_custom_call" | custom-call | tf_op jit(solution)/shard_map/pallas_call | solution.py:556

commit v5 on v4

--- a/solution.py
+++ b/solution.py
@@ -118,6 +118,13 @@
 
     partner = (chip * 2 + 1 - core, my_head)
 
+    groups = nh // 2
+    group, bit = my_head // 2, lax.rem(my_head, 2)
+    side = (me, group * 2 + 1 - bit)
+
+    def at_group(k):
+        return (me, lax.rem(group + k, groups) * 2 + bit)
+
     def at_head(k):
         return (me, lax.rem(my_head + k, nh))
 
@@ -175,6 +182,7 @@
         loads[name] = pltpu.make_async_copy(src, dst, load_sem.at[i])
         loads[name].start()
 
+    order = one_hot(token_order, TILE_H * TILE_W)
     loads["cot"].wait()
     cot_all[my_head] = cot_ref[...]
     pl.semaphore_wait(barrier, n + nh - 2)
@@ -182,7 +190,6 @@
         send_head(0, k, cot_ref, cot_all.at[my_head], at_head(k)) for k in range(1, nh)
     ]
 
-    order = one_hot(token_order, TILE_H * TILE_W)
     loads["tokens"].wait()
     tokens = mm(order, tokens_ref[...])
     center = tokens - jnp.mean(tokens, axis=-1, keepdims=True)
@@ -291,15 +298,15 @@
     keys = kv_all[0]
     values = kv_all[1]
     scale = HEAD_DIM ** (-0.5)
-    exp_scores = jnp.exp(mm(q_rows, keys, (1, 1)) * scale)
-    row_total = jnp.sum(exp_scores, axis=-1, keepdims=True)
+    exp_scores = jnp.exp(mm(keys, q_rows, (1, 1)) * scale)
+    row_total = jnp.sum(exp_scores, axis=0, keepdims=True)
     probs = (exp_scores / row_total).astype(BF16)
-    dprobs = mm(g_rows, values, (1, 1))
+    dprobs = mm(values, g_rows, (1, 1))
     probs_wide = probs.astype(F32)
-    row_delta = jnp.sum(probs_wide * dprobs, axis=-1, keepdims=True)
+    row_delta = jnp.sum(probs_wide * dprobs, axis=0, keepdims=True)
     d_scores = (scale * probs_wide * (dprobs - row_delta)).astype(BF16)
-    key_grad = mm(d_scores, q_rows, (0, 0))
-    value_grad = mm(probs, g_rows, (0, 0))
+    key_grad = mm(d_scores, q_rows)
+    value_grad = mm(probs, g_rows)
     kvg_send[0] = key_grad.astype(BF16)
     kvg_send[1] = value_grad.astype(BF16)
     kvg_copies = [
@@ -313,7 +320,7 @@
         for k in range(1, n)
     ]
 
-    attended = (from_heads(mm(probs, values)) + queries_wide).astype(BF16)
+    attended = (from_heads(mm(probs, values, (0, 0))) + queries_wide).astype(BF16)
     head_part = mm(mm(cells_back, attended).astype(BF16), proj_ref[...])
     for h in range(nh):
         hp_send[h] = head_part[:, h * chans : (h + 1) * chans].astype(BF16)
@@ -322,7 +329,7 @@
         for k in range(1, nh)
     ]
 
-    query_grad = from_heads(mm(d_scores, keys)) + d_attended
+    query_grad = from_heads(mm(d_scores, keys, (0, 0))) + d_attended
     spread = []
     for s in range(16):
         a, b = s // 4, s % 4
@@ -419,22 +426,22 @@
         send_tile(6, 1, gb_send.at[rows((1 - core) * half_b, half_b)], gb_pair, partner)
     ]
 
+    pooled_input = mm(cells_back, pooled_input).astype(BF16)
+    skipped = mm(pooled_input, skip_ref[...], (1, 1))
+    arrived(dp_copies)
+    d_pooled = dp_send[my_head * 2 // nh].astype(F32)
+    for k in range(1, nh):
+        d_pooled = d_pooled + dp_recv[k].astype(F32)
+    d_pooled = d_pooled * 0.25
+
     gb_copies = fold(7, gb_pairs, gb_send, gb_pair, gb_part, gb_recv, share_b)
     ga_shares, ga_relays = reduce_and_share(4, ga_copies, ga_part, ga_recv, ga_out, share_a)
 
-    pooled_input = mm(cells_back, pooled_input).astype(BF16)
-    skipped = mm(pooled_input, skip_ref[...], (1, 1))
     arrived(hp_copies)
     summed = hp_send[my_head].astype(F32)
     for k in range(1, nh):
         summed = summed + hp_recv[k].astype(F32)
     block_out_ref[...] = (summed + skipped).astype(BF16)
-
-    arrived(dp_copies)
-    d_pooled = dp_send[my_head * 2 // nh].astype(F32)
-    for k in range(1, nh):
-        d_pooled = d_pooled + dp_recv[k].astype(F32)
-    d_pooled = d_pooled * 0.25
 
     def share_input(half):
         arrived(dn_copies[half])
@@ -451,17 +458,28 @@
         )
         cell = d_pooled[half * SLAB : (half + 1) * SLAB]
         ig_all[mine, :] = (back + jnp.concatenate([cell, cell], axis=0)).astype(BF16)
-        return [
-            send_head(5 + half, k, ig_all.at[mine], ig_all.at[mine], at_head(k))
-            for k in range(1, nh)
+        far = [
+            send_head(5 + half, k, ig_all.at[mine], ig_all.at[mine], at_group(k))
+            for k in range(1, groups)
         ]
-
-    ig_copies = share_input(0)
+        return far, [send_head(7 + half, 0, ig_all.at[mine], ig_all.at[mine], side)]
+
+    def relay_input(half, far, near):
+        for k in range(1, groups):
+            arrived(far[k - 1 : k])
+            owner = lax.rem(group + groups - k, groups) * 2 + bit
+            there = rows(owner * share_h + half * piece, piece)
+            near.append(send_head(7 + half, k, ig_all.at[there], ig_all.at[there], side))
+
+    first_far, first_near = share_input(0)
     gb_shares, gb_relays = reduce_and_share(8, gb_copies, gb_part, gb_recv, gb_out, share_b)
-    ig_copies += share_input(1)
+    last_far, last_near = share_input(1)
     relay(5, ga_shares, ga_relays, ga_out, share_a)
+    relay_input(0, first_far, first_near)
     relay(9, gb_shares, gb_relays, gb_out, share_b)
-    arrived(ig_copies)
+    relay_input(1, last_far, last_near)
+    arrived(first_near)
+    arrived(last_near)
     arrived(ga_relays)
     arrived(gb_relays)
     for copy in started:
@@ -546,8 +564,8 @@
             pltpu.SemaphoreType.DMA((9,)),
             pltpu.SemaphoreType.DMA((10, n)),
             pltpu.SemaphoreType.DMA((10, n)),
-            pltpu.SemaphoreType.DMA((7, nh)),
-            pltpu.SemaphoreType.DMA((7, nh)),
+            pltpu.SemaphoreType.DMA((9, nh)),
+            pltpu.SemaphoreType.DMA((9, nh)),
         ],
         compiler_params=pltpu.CompilerParams(
             collective_id=0, has_side_effects=True, vmem_limit_bytes=40 * 1024 * 1024

time: 31.3 us -> 33.1 us (1.058)
  Pallas kernels: 30.5 us -> 32.3 us
    pallas_call x1, Pallas kernels: 29.1 us -> 30.9 us  [local(): pl.pallas_call(functools.partial(kernel, n, nh, share_a, share_b), out_sh...]
where the time goes in v5:
time: 33.1 us; the launch traced here: 33 us
  Pallas kernels  32.3 us (98%)
  between operations  0.64 us (2%)
    pallas_call x1, Pallas kernels, local(): pl.pallas_call(functools.partial(kernel, n, nh, share_a, share_b), out_sh...  30.9 us
    pallas_call x1, Pallas kernels, local(): pl.pallas_call(finish, out_shape=(jax.ShapeDtypeStruct(cot.shape, BF16),...  1.45 us

profile of v5, /device:TPU:0, one launch (start us, length us, event | category | flops | bytes accessed | tf_op | source)
XLA Modules:
  0.0 33.0 jit_solution(7428885393356548598)
XLA Ops:
  0.6 30.9 %shard_map.120 = (bf16[64,192]{1,0:T(8,128)(2,1)S(1)}, bf16[256,384]{1,0:T(8,128)(2,1)S(1)}, bf16[640,384]{1,0:T(8,128)(2,1)S(1)}, bf16[384,384]{1,0:T(8,128)(2,1)S(1)}) custom-call(bf16[256,384]{1,0:T(8,128)(2,1)} %tokens_hbm.1, f32[384]{0:T(512)} %gain_hbm.1, bf16[3,192,384]{2,1,0:T(8,128)(2,1)} %qkv_hbm.1, bf16[4,192]{1,0:T(4,128)(2,1)} %qpool_hbm.1, ...), custom_call_target="tpu_custom_call" | custom-call | tf_op jit(solution)/shard_map/pallas_call | solution.py:532
  31.5 1.5 %shard_map.121 = (bf16[64,192]{1,0:T(8,128)(2,1)}, bf16[256,384]{1,0:T(8,128)(2,1)}, f32[3,192,384]{2,1,0:T(8,128)}, f32[192,768]{1,0:T(8,128)}) custom-call(bf16[64,192]{1,0:T(8,128)(2,1)S(1)} %get-tuple-element.8.block_ref, bf16[256,384]{1,0:T(8,128)(2,1)S(1)} %get-tuple-element.9.ig_ref, bf16[640,384]{1,0:T(8,128)(2,1)S(1)} %get-tuple-element.10.ga_ref, ...), custom_call_target="tpu_custom_call" | custom-call | tf_op jit(solution)/shard_map/pallas_call | solution.py:574

commit v6 on v4

--- a/solution.py
+++ b/solution.py
@@ -89,8 +89,6 @@
     ga_part,
     ga_recv,
     gb_send,
-    gb_pair,
-    gb_part,
     gb_recv,
     dn_send,
     dn_recv,
@@ -175,6 +173,7 @@
         loads[name] = pltpu.make_async_copy(src, dst, load_sem.at[i])
         loads[name].start()
 
+    order = one_hot(token_order, TILE_H * TILE_W)
     loads["cot"].wait()
     cot_all[my_head] = cot_ref[...]
     pl.semaphore_wait(barrier, n + nh - 2)
@@ -182,7 +181,6 @@
         send_head(0, k, cot_ref, cot_all.at[my_head], at_head(k)) for k in range(1, nh)
     ]
 
-    order = one_hot(token_order, TILE_H * TILE_W)
     loads["tokens"].wait()
     tokens = mm(order, tokens_ref[...])
     center = tokens - jnp.mean(tokens, axis=-1, keepdims=True)
@@ -291,15 +289,15 @@
     keys = kv_all[0]
     values = kv_all[1]
     scale = HEAD_DIM ** (-0.5)
-    exp_scores = jnp.exp(mm(q_rows, keys, (1, 1)) * scale)
-    row_total = jnp.sum(exp_scores, axis=-1, keepdims=True)
+    exp_scores = jnp.exp(mm(keys, q_rows, (1, 1)) * scale)
+    row_total = jnp.sum(exp_scores, axis=0, keepdims=True)
     probs = (exp_scores / row_total).astype(BF16)
-    dprobs = mm(g_rows, values, (1, 1))
+    dprobs = mm(values, g_rows, (1, 1))
     probs_wide = probs.astype(F32)
-    row_delta = jnp.sum(probs_wide * dprobs, axis=-1, keepdims=True)
+    row_delta = jnp.sum(probs_wide * dprobs, axis=0, keepdims=True)
     d_scores = (scale * probs_wide * (dprobs - row_delta)).astype(BF16)
-    key_grad = mm(d_scores, q_rows, (0, 0))
-    value_grad = mm(probs, g_rows, (0, 0))
+    key_grad = mm(d_scores, q_rows)
+    value_grad = mm(probs, g_rows)
     kvg_send[0] = key_grad.astype(BF16)
     kvg_send[1] = value_grad.astype(BF16)
     kvg_copies = [
@@ -313,7 +311,7 @@
         for k in range(1, n)
     ]
 
-    attended = (from_heads(mm(probs, values)) + queries_wide).astype(BF16)
+    attended = (from_heads(mm(probs, values, (0, 0))) + queries_wide).astype(BF16)
     head_part = mm(mm(cells_back, attended).astype(BF16), proj_ref[...])
     for h in range(nh):
         hp_send[h] = head_part[:, h * chans : (h + 1) * chans].astype(BF16)
@@ -322,7 +320,7 @@
         for k in range(1, nh)
     ]
 
-    query_grad = from_heads(mm(d_scores, keys)) + d_attended
+    query_grad = from_heads(mm(d_scores, keys, (0, 0))) + d_attended
     spread = []
     for s in range(16):
         a, b = s // 4, s % 4
@@ -338,7 +336,7 @@
     filled = (halves + 1) * chans
     if ga_send.shape[0] > filled:
         ga_send[filled:, :] = jnp.zeros((ga_send.shape[0] - filled, wide), BF16)
-    half_a, half_b = chips * share_a, chips * share_b
+    half_a = chips * share_a
     ga_pairs = [
         send_tile(2, 1, ga_send.at[rows((1 - core) * half_a, half_a)], ga_pair, partner)
     ]
@@ -415,26 +413,32 @@
     filled = 2 * chans
     if gb_send.shape[0] > filled:
         gb_send[filled:, :] = jnp.zeros((gb_send.shape[0] - filled, wide), BF16)
-    gb_pairs = [
-        send_tile(6, 1, gb_send.at[rows((1 - core) * half_b, half_b)], gb_pair, partner)
-    ]
-
-    gb_copies = fold(7, gb_pairs, gb_send, gb_pair, gb_part, gb_recv, share_b)
-    ga_shares, ga_relays = reduce_and_share(4, ga_copies, ga_part, ga_recv, ga_out, share_a)
+    gb_copies = [
+        send_tile(
+            6,
+            k,
+            gb_send.at[rows(lax.rem(me + k, n) * share_b, share_b)],
+            gb_recv.at[k],
+            at_tile(k),
+        )
+        for k in range(1, n)
+    ]
 
     pooled_input = mm(cells_back, pooled_input).astype(BF16)
     skipped = mm(pooled_input, skip_ref[...], (1, 1))
+    arrived(dp_copies)
+    d_pooled = dp_send[my_head * 2 // nh].astype(F32)
+    for k in range(1, nh):
+        d_pooled = d_pooled + dp_recv[k].astype(F32)
+    d_pooled = d_pooled * 0.25
+
+    ga_shares, ga_relays = reduce_and_share(4, ga_copies, ga_part, ga_recv, ga_out, share_a)
+
     arrived(hp_copies)
     summed = hp_send[my_head].astype(F32)
     for k in range(1, nh):
         summed = summed + hp_recv[k].astype(F32)
     block_out_ref[...] = (summed + skipped).astype(BF16)
-
-    arrived(dp_copies)
-    d_pooled = dp_send[my_head * 2 // nh].astype(F32)
-    for k in range(1, nh):
-        d_pooled = d_pooled + dp_recv[k].astype(F32)
-    d_pooled = d_pooled * 0.25
 
     def share_input(half):
         arrived(dn_copies[half])
@@ -457,13 +461,20 @@
         ]
 
     ig_copies = share_input(0)
-    gb_shares, gb_relays = reduce_and_share(8, gb_copies, gb_part, gb_recv, gb_out, share_b)
+    arrived(gb_copies)
+    mine = rows(me * share_b, share_b)
+    total = gb_send[mine, :].astype(F32)
+    for k in range(1, n):
+        total = total + gb_recv[k].astype(F32)
+    gb_out[mine, :] = total.astype(BF16)
+    gb_shares = [
+        send_tile(7, k, gb_out.at[mine], gb_out.at[mine], at_tile(k)) for k in range(1, n)
+    ]
     ig_copies += share_input(1)
     relay(5, ga_shares, ga_relays, ga_out, share_a)
-    relay(9, gb_shares, gb_relays, gb_out, share_b)
     arrived(ig_copies)
     arrived(ga_relays)
-    arrived(gb_relays)
+    arrived(gb_shares)
     for copy in started:
         copy.wait_send()
 
@@ -536,16 +547,14 @@
             pltpu.VMEM((n // 2 * share_a, wide), BF16),
             pltpu.VMEM((n // 2, share_a, wide), BF16),
             pltpu.VMEM((n * share_b, wide), BF16),
-            pltpu.VMEM((n // 2 * share_b, wide), BF16),
-            pltpu.VMEM((n // 2 * share_b, wide), BF16),
-            pltpu.VMEM((n // 2, share_b, wide), BF16),
+            pltpu.VMEM((n, share_b, wide), BF16),
             pltpu.VMEM((count, wide), BF16),
             pltpu.VMEM((nh, share_h, wide), BF16),
             pltpu.VMEM((count, wide), F32),
             pltpu.VMEM((count, 128), F32),
             pltpu.SemaphoreType.DMA((9,)),
-            pltpu.SemaphoreType.DMA((10, n)),
-            pltpu.SemaphoreType.DMA((10, n)),
+            pltpu.SemaphoreType.DMA((8, n)),
+            pltpu.SemaphoreType.DMA((8, n)),
             pltpu.SemaphoreType.DMA((7, nh)),
             pltpu.SemaphoreType.DMA((7, nh)),
         ],

time: 31.3 us -> 31.2 us (level)
  no operation moved by 1% of the time
where the time goes in v6:
time: 31.2 us; the launch traced here: 31 us
  Pallas kernels  30.4 us (97%)
  between operations  0.64 us (2%)
    pallas_call x1, Pallas kernels, local(): pl.pallas_call(functools.partial(kernel, n, nh, share_a, share_b), out_sh...  28.9 us
    pallas_call x1, Pallas kernels, local(): pl.pallas_call(finish, out_shape=(jax.ShapeDtypeStruct(cot.shape, BF16),...  1.45 us

profile of v6, /device:TPU:0, one launch (start us, length us, event | category | flops | bytes accessed | tf_op | source)
XLA Modules:
  0.0 31.0 jit_solution(16785772164214140766)
XLA Ops:
  0.6 28.9 %shard_map.120 = (bf16[64,192]{1,0:T(8,128)(2,1)S(1)}, bf16[256,384]{1,0:T(8,128)(2,1)S(1)}, bf16[640,384]{1,0:T(8,128)(2,1)S(1)}, bf16[384,384]{1,0:T(8,128)(2,1)S(1)}) custom-call(bf16[256,384]{1,0:T(8,128)(2,1)} %tokens_hbm.1, f32[384]{0:T(512)} %gain_hbm.1, bf16[3,192,384]{2,1,0:T(8,128)(2,1)} %qkv_hbm.1, bf16[4,192]{1,0:T(4,128)(2,1)} %qpool_hbm.1, ...), custom_call_target="tpu_custom_call" | custom-call | tf_op jit(solution)/shard_map/pallas_call | solution.py:525
  29.6 1.5 %shard_map.121 = (bf16[64,192]{1,0:T(8,128)(2,1)}, bf16[256,384]{1,0:T(8,128)(2,1)}, f32[3,192,384]{2,1,0:T(8,128)}, f32[192,768]{1,0:T(8,128)}) custom-call(bf16[64,192]{1,0:T(8,128)(2,1)S(1)} %get-tuple-element.8.block_ref, bf16[256,384]{1,0:T(8,128)(2,1)S(1)} %get-tuple-element.9.ig_ref, bf16[640,384]{1,0:T(8,128)(2,1)S(1)} %get-tuple-element.10.ga_ref, ...), custom_call_target="tpu_custom_call" | custom-call | tf_op jit(solution)/shard_map/pallas_call | solution.py:565

commit v7 on v6

--- a/solution.py
+++ b/solution.py
@@ -382,8 +382,6 @@
             there = place(k, share)
             relays.append(send_tile(stage, k, out.at[there], out.at[there], partner))
 
-    ga_copies = fold(3, ga_pairs, ga_send, ga_pair, ga_part, ga_recv, share_a)
-
     arrived(kvg_copies)
     d_fields = []
     for j, pool, own in ((0, kpool, key_grad), (1, vpool, value_grad)):
@@ -408,6 +406,7 @@
         ]
         for half in range(2)
     ]
+    ga_copies = fold(3, ga_pairs, ga_send, ga_pair, ga_part, ga_recv, share_a)
     for j in range(2):
         gb_send[j * chans : (j + 1) * chans, :] = mm(d_fields[j], normed, (0, 0)).astype(BF16)
     filled = 2 * chans
@@ -432,13 +431,6 @@
         d_pooled = d_pooled + dp_recv[k].astype(F32)
     d_pooled = d_pooled * 0.25
 
-    ga_shares, ga_relays = reduce_and_share(4, ga_copies, ga_part, ga_recv, ga_out, share_a)
-
-    arrived(hp_copies)
-    summed = hp_send[my_head].astype(F32)
-    for k in range(1, nh):
-        summed = summed + hp_recv[k].astype(F32)
-    block_out_ref[...] = (summed + skipped).astype(BF16)
 
     def share_input(half):
         arrived(dn_copies[half])
@@ -461,6 +453,8 @@
         ]
 
     ig_copies = share_input(0)
+    ga_shares, ga_relays = reduce_and_share(4, ga_copies, ga_part, ga_recv, ga_out, share_a)
+    ig_copies += share_input(1)
     arrived(gb_copies)
     mine = rows(me * share_b, share_b)
     total = gb_send[mine, :].astype(F32)
@@ -470,7 +464,12 @@
     gb_shares = [
         send_tile(7, k, gb_out.at[mine], gb_out.at[mine], at_tile(k)) for k in range(1, n)
     ]
-    ig_copies += share_input(1)
+    arrived(hp_copies)
+    summed = hp_send[my_head].astype(F32)
+    for k in range(1, nh):
+        summed = summed + hp_recv[k].astype(F32)
+    block_out_ref[...] = (summed + skipped).astype(BF16)
+
     relay(5, ga_shares, ga_relays, ga_out, share_a)
     arrived(ig_copies)
     arrived(ga_relays)

time: 31.2 us -> 31.7 us (1.016)
  Pallas kernels: 30.4 us -> 30.9 us
    pallas_call x1, Pallas kernels: 28.9 us -> 29.4 us  [local(): pl.pallas_call(functools.partial(kernel, n, nh, share_a, share_b), out_sh...]
where the time goes in v7:
time: 31.7 us; the launch traced here: 31.5 us
  Pallas kernels  30.9 us (97%)
  between operations  0.64 us (2%)
    pallas_call x1, Pallas kernels, local(): pl.pallas_call(functools.partial(kernel, n, nh, share_a, share_b), out_sh...  29.4 us
    pallas_call x1, Pallas kernels, local(): pl.pallas_call(finish, out_shape=(jax.ShapeDtypeStruct(cot.shape, BF16),...  1.46 us

profile of v7, /device:TPU:0, one launch (start us, length us, event | category | flops | bytes accessed | tf_op | source)
XLA Modules:
  0.0 31.5 jit_solution(17353831787809908063)
XLA Ops:
  0.6 29.4 %shard_map.120 = (bf16[64,192]{1,0:T(8,128)(2,1)S(1)}, bf16[256,384]{1,0:T(8,128)(2,1)S(1)}, bf16[640,384]{1,0:T(8,128)(2,1)S(1)}, bf16[384,384]{1,0:T(8,128)(2,1)S(1)}) custom-call(bf16[256,384]{1,0:T(8,128)(2,1)} %tokens_hbm.1, f32[384]{0:T(512)} %gain_hbm.1, bf16[3,192,384]{2,1,0:T(8,128)(2,1)} %qkv_hbm.1, bf16[4,192]{1,0:T(4,128)(2,1)} %qpool_hbm.1, ...), custom_call_target="tpu_custom_call" | custom-call | tf_op jit(solution)/shard_map/pallas_call | solution.py:524
  30.0 1.5 %shard_map.121 = (bf16[64,192]{1,0:T(8,128)(2,1)}, bf16[256,384]{1,0:T(8,128)(2,1)}, f32[3,192,384]{2,1,0:T(8,128)}, f32[192,768]{1,0:T(8,128)}) custom-call(bf16[64,192]{1,0:T(8,128)(2,1)S(1)} %get-tuple-element.8.block_ref, bf16[256,384]{1,0:T(8,128)(2,1)S(1)} %get-tuple-element.9.ig_ref, bf16[640,384]{1,0:T(8,128)(2,1)S(1)} %get-tuple-element.10.ga_ref, ...), custom_call_target="tpu_custom_call" | custom-call | tf_op jit(solution)/shard_map/pallas_call | solution.py:564

commit v8 on v5

--- a/solution.py
+++ b/solution.py
@@ -118,13 +118,6 @@
 
     partner = (chip * 2 + 1 - core, my_head)
 
-    groups = nh // 2
-    group, bit = my_head // 2, lax.rem(my_head, 2)
-    side = (me, group * 2 + 1 - bit)
-
-    def at_group(k):
-        return (me, lax.rem(group + k, groups) * 2 + bit)
-
     def at_head(k):
         return (me, lax.rem(my_head + k, nh))
 
@@ -458,28 +451,17 @@
         )
         cell = d_pooled[half * SLAB : (half + 1) * SLAB]
         ig_all[mine, :] = (back + jnp.concatenate([cell, cell], axis=0)).astype(BF16)
-        far = [
-            send_head(5 + half, k, ig_all.at[mine], ig_all.at[mine], at_group(k))
-            for k in range(1, groups)
+        return [
+            send_head(5 + half, k, ig_all.at[mine], ig_all.at[mine], at_head(k))
+            for k in range(1, nh)
         ]
-        return far, [send_head(7 + half, 0, ig_all.at[mine], ig_all.at[mine], side)]
-
-    def relay_input(half, far, near):
-        for k in range(1, groups):
-            arrived(far[k - 1 : k])
-            owner = lax.rem(group + groups - k, groups) * 2 + bit
-            there = rows(owner * share_h + half * piece, piece)
-            near.append(send_head(7 + half, k, ig_all.at[there], ig_all.at[there], side))
-
-    first_far, first_near = share_input(0)
+
+    ig_copies = share_input(0)
     gb_shares, gb_relays = reduce_and_share(8, gb_copies, gb_part, gb_recv, gb_out, share_b)
-    last_far, last_near = share_input(1)
+    ig_copies += share_input(1)
     relay(5, ga_shares, ga_relays, ga_out, share_a)
-    relay_input(0, first_far, first_near)
     relay(9, gb_shares, gb_relays, gb_out, share_b)
-    relay_input(1, last_far, last_near)
-    arrived(first_near)
-    arrived(last_near)
+    arrived(ig_copies)
     arrived(ga_relays)
     arrived(gb_relays)
     for copy in started:
@@ -564,8 +546,8 @@
             pltpu.SemaphoreType.DMA((9,)),
             pltpu.SemaphoreType.DMA((10, n)),
             pltpu.SemaphoreType.DMA((10, n)),
-            pltpu.SemaphoreType.DMA((9, nh)),
-            pltpu.SemaphoreType.DMA((9, nh)),
+            pltpu.SemaphoreType.DMA((7, nh)),
+            pltpu.SemaphoreType.DMA((7, nh)),
         ],
         compiler_params=pltpu.CompilerParams(
             collective_id=0, has_side_effects=True, vmem_limit_bytes=40 * 1024 * 1024

time: 33.1 us -> 31.2 us (0.943)
  Pallas kernels: 32.3 us -> 30.4 us
    pallas_call x1, Pallas kernels: 30.9 us -> 28.9 us  [local(): pl.pallas_call(functools.partial(kernel, n, nh, share_a, share_b), out_sh...]
where the time goes in v8:
time: 31.2 us; the launch traced here: 31 us
  Pallas kernels  30.4 us (97%)
  between operations  0.64 us (2%)
    pallas_call x1, Pallas kernels, local(): pl.pallas_call(functools.partial(kernel, n, nh, share_a, share_b), out_sh...  28.9 us
    pallas_call x1, Pallas kernels, local(): pl.pallas_call(finish, out_shape=(jax.ShapeDtypeStruct(cot.shape, BF16),...  1.46 us

profile of v8, /device:TPU:0, one launch (start us, length us, event | category | flops | bytes accessed | tf_op | source)
XLA Modules:
  0.0 31.0 jit_solution(13452104763649170825)
XLA Ops:
  0.6 28.9 %shard_map.120 = (bf16[64,192]{1,0:T(8,128)(2,1)S(1)}, bf16[256,384]{1,0:T(8,128)(2,1)S(1)}, bf16[640,384]{1,0:T(8,128)(2,1)S(1)}, bf16[384,384]{1,0:T(8,128)(2,1)S(1)}) custom-call(bf16[256,384]{1,0:T(8,128)(2,1)} %tokens_hbm.1, f32[384]{0:T(512)} %gain_hbm.1, bf16[3,192,384]{2,1,0:T(8,128)(2,1)} %qkv_hbm.1, bf16[4,192]{1,0:T(4,128)(2,1)} %qpool_hbm.1, ...), custom_call_target="tpu_custom_call" | custom-call | tf_op jit(solution)/shard_map/pallas_call | solution.py:514
  29.6 1.5 %shard_map.121 = (bf16[64,192]{1,0:T(8,128)(2,1)}, bf16[256,384]{1,0:T(8,128)(2,1)}, f32[3,192,384]{2,1,0:T(8,128)}, f32[192,768]{1,0:T(8,128)}) custom-call(bf16[64,192]{1,0:T(8,128)(2,1)S(1)} %get-tuple-element.8.block_ref, bf16[256,384]{1,0:T(8,128)(2,1)S(1)} %get-tuple-element.9.ig_ref, bf16[640,384]{1,0:T(8,128)(2,1)S(1)} %get-tuple-element.10.ga_ref, ...), custom_call_target="tpu_custom_call" | custom-call | tf_op jit(solution)/shard_map/pallas_call | solution.py:556
